TPU v7x, 128 devices: a whole 4x4x4 slice. The times are simulated.
128 devices in a mesh: gy: 8 (over y, core), gz: 16 (over x, z).
Axes of the slice: x: 4, y: 4, z: 4, core: 2. Of those that a mesh axis runs over, the one named last changes fastest.
Arguments:
- velocity: float32 [1536, 147456], P('gz', 'gy'), may hold values from -6 to 6
Outputs:
- deriv_y: float32 [1536, 147456], P('gz', 'gy')
- deriv_z: float32 [1536, 147456], P('gz', 'gy')
All inputs are finite; a program needn't handle non-finite values.
Results may differ from a plain program's by a relative error of at most 0.00007.
Values sent between devices are 32-bit elements; how exact they have to be, the bound alone decides.
No kernel may reach another device: no remote copies, remote signals or barrier semaphores. Data moves between devices by JAX's collectives and lax.ppermute only.
A program may use at most 192 MiB of HBM per device.

v0:
```python
import functools

import jax
import jax.numpy as jnp
import ml_dtypes
import numpy as np
from jax import lax
from jax.experimental import pallas as pl
from jax.experimental.pallas import tpu as pltpu
from jax.sharding import PartitionSpec as P

X = 96
ROOT = (5.0**0.5 - 3.0) / 2.0
EDGE = 1.0 / 12.0
GAIN = 25.0 / 12.0
LANES = 128
BLOCK = 4 * X
Q = ROOT**4
F32 = jnp.float32


def lane_index(rows):
    return lax.broadcasted_iota(jnp.int32, (rows, LANES), 1)


def rolled(x, by):
    return pltpu.roll(x, by, 1)


def summarize(u_hbm, u_v, zf, zb, yf, yb, acc_f, acc_b, sems, *, chunks):
    rows, width = u_v.shape
    wide = width // chunks
    per = wide // BLOCK

    def copy(c):
        lanes = pl.ds(c * wide, wide)
        return pltpu.make_async_copy(u_hbm.at[:, lanes], u_v.at[:, lanes], sems.at[c])

    for c in range(chunks):
        copy(c).start()
    sub = lax.broadcasted_iota(jnp.int32, (8, wide), 0)
    w_f = jnp.zeros((8, wide), F32)
    w_b = jnp.zeros((8, wide), F32)
    for r in range(8):
        w_f = jnp.where(sub == r, np.float32(ROOT ** (7 - r)), w_f)
        w_b = jnp.where(sub == r, np.float32(ROOT**r), w_b)
    for c in range(chunks):
        copy(c).wait()
        z_f = z_b = None
        for g in range(rows // 8):
            rs = slice(8 * g, 8 * g + 8)
            x = u_v[rs, c * wide : (c + 1) * wide]
            if g == 0:
                z_f, z_b = x, x
            else:
                z_f = z_f * np.float32(ROOT**8) + x
                z_b = z_b + x * np.float32(ROOT ** (8 * g))
            parts = [x[:, b * BLOCK : (b + 1) * BLOCK] for b in range(per)]
            y_f = acc_f[rs, :] if c else None
            for part in parts:
                y_f = part if y_f is None else y_f * np.float32(Q) + part
            acc_f[rs, :] = y_f
            y_b = None
            for part in reversed(parts):
                y_b = part if y_b is None else y_b * np.float32(Q) + part
            acc_b[rs, :] = acc_b[rs, :] + y_b * np.float32(Q ** (per * c)) if c else y_b
        lanes = slice(c * wide, (c + 1) * wide)
        zf[0:1, lanes] = jnp.sum(z_f * w_f, axis=0, keepdims=True)
        zb[0:1, lanes] = jnp.sum(z_b * w_b, axis=0, keepdims=True)
        zf[1:2, lanes] = u_v[rows - 1 : rows, lanes]
        zb[1:2, lanes] = u_v[0:1, lanes]
    lane = lane_index(8)
    for g in range(rows // 8):
        rs = slice(8 * g, 8 * g + 8)
        v0, v1, v2 = (acc_f[rs, k * LANES : (k + 1) * LANES] for k in range(3))
        s = v2 + np.float32(ROOT) * jnp.where(lane < 96, rolled(v1, 96), rolled(v2, 96))
        s = s + np.float32(ROOT**2) * jnp.where(lane < 64, rolled(v0, 64), rolled(v1, 64))
        s = s + np.float32(ROOT**3) * rolled(v0, 32)
        yf[rs, 0:LANES] = jnp.where(lane < 32, np.float32(0), s)
        yf[rs, LANES:] = u_v[rs, width - LANES :]
        v0, v1, v2 = (acc_b[rs, k * LANES : (k + 1) * LANES] for k in range(3))
        s = v0 + np.float32(ROOT) * jnp.where(lane < 32, rolled(v0, 32), rolled(v1, 32))
        s = s + np.float32(ROOT**2) * jnp.where(lane < 64, rolled(v1, 64), rolled(v2, 64))
        s = s + np.float32(ROOT**3) * rolled(v2, 96)
        yb[rs, 0:LANES] = jnp.where(lane < 96, s, np.float32(0))
        yb[rs, LANES:] = u_v[rs, 0:LANES]


def add(a, b):
    return b if a is None else a if b is None else a + b


def sub(a, b):
    return a if b is None else -b if a is None else a - b


def times(a, k):
    return None if a is None else a * np.float32(k)


def derive_y(u_v, low, high, dy, ybuf, obuf, sems, *, tall):
    rows, width = u_v.shape
    count = width // LANES
    lane = lane_index(tall)
    scale = GAIN * Q

    def step(i, carry):
        rs = pl.ds(pl.multiple_of(i * tall, tall), tall)
        s_low, s_high = low[rs, 0:LANES], high[rs, 0:LANES]
        t_low, t_high = low[rs, LANES:], high[rs, LANES:]

        @functools.cache
        def u(t):
            if 0 <= t < count:
                return u_v[rs, t * LANES : (t + 1) * LANES]
            return s_low if t == -1 else s_high if t == count else None

        @functools.cache
        def turn(t, by):
            return None if u(t) is None else rolled(u(t), by)

        def merge(below, a, b):
            if a is None and b is None:
                return None
            zero = jnp.zeros((tall, LANES), F32)
            return jnp.where(lane < below, zero if a is None else a, zero if b is None else b)

        @functools.cache
        def u1(t):
            return merge(96, turn(t - 1, 96), turn(t, 96))

        @functools.cache
        def u2(t):
            return merge(64, turn(t - 2, 64), turn(t - 1, 64))

        @functools.cache
        def u3(t):
            return merge(32, turn(t - 3, 32), turn(t - 2, 32))

        y = {-4: times(s_low, -scale)}
        for t in range(-3, count + 3):
            d1 = sub(u3(t + 3), u1(t))
            d2 = sub(u2(t + 3), u2(t))
            d3 = sub(u1(t + 3), u3(t))
            d4 = sub(u(t + 3), u(t - 3))
            f = sub(times(d1, 18 * scale), times(d2, 7 * scale))
            f = sub(add(f, times(d3, 3 * scale)), times(d4, scale))
            y[t] = add(f, times(y.pop(t - 3, None), Q))
            if 0 <= t < count:
                ybuf[:, t * LANES : (t + 1) * LANES] = y[t]
                if t == 0:
                    d1 = u3(t + 3) - jnp.where(lane < 96, rolled(t_low, 96), turn(t, 96))
                if t == count - 1:
                    d1 = jnp.where(lane < 32, turn(t, 32), rolled(t_high, 32)) - u1(t)
                obuf[rs, t * LANES : (t + 1) * LANES] = d1 * np.float32(EDGE)
        z = {}
        for k in range(3):
            tail = times(y[count + k], Q)
            if k == 0:
                tail = tail + s_high * np.float32(scale)
            z[count + k] = y[count + k] + tail * np.float32(Q / (1 - Q * Q))
        for t in reversed(range(count)):
            ls = slice(t * LANES, (t + 1) * LANES)
            z[t] = ybuf[:, ls] + z.pop(t + 3) * np.float32(Q)
            obuf[rs, ls] = obuf[rs, ls] + z[t]
        pltpu.make_async_copy(obuf.at[rs], dy.at[rs], sems.at[i]).start()
        return carry

    lax.fori_loop(0, rows // tall, step, 0)

    def finish(i, carry):
        rs = pl.ds(pl.multiple_of(i * tall, tall), tall)
        pltpu.make_async_copy(obuf.at[rs], dy.at[rs], sems.at[i]).wait()
        return carry

    lax.fori_loop(0, rows // tall, finish, 0)


def halves(x):
    high = x.astype(jnp.bfloat16)
    return high, (x - high.astype(F32)).astype(jnp.bfloat16)


def z_matrix(rows):
    at = np.arange(rows)
    k = at[:, None] - at[None, :]
    own = GAIN * np.sign(k) * ROOT ** np.abs(k) - EDGE * ((k == 1).astype(float) - (k == -1))
    halo = np.zeros((rows, 16))
    halo[:, 0] = GAIN * ROOT ** (at + 1.0)
    halo[0, 1] = -EDGE
    halo[:, 2] = -GAIN * ROOT ** (rows - at * 1.0)
    halo[rows - 1, 3] = EDGE
    whole = np.concatenate([own, own, halo, halo], axis=1).astype(np.float32)
    high = whole.astype(ml_dtypes.bfloat16)
    low = (whole - high.astype(np.float32)).astype(ml_dtypes.bfloat16)
    return np.concatenate([high, low], axis=0)


def derive_z(u_v, low, high, matrix, dz, rhs, halo, obuf, sems, *, chunks):
    rows, width = u_v.shape
    wide = width // chunks
    halo[...] = jnp.zeros(halo.shape, F32)

    def step(i, carry):
        ls = pl.ds(pl.multiple_of(i * wide, wide), wide)
        halo[0:2, :] = low[:, ls]
        halo[2:4, :] = high[:, ls]
        rhs[0:rows, :], rhs[rows : 2 * rows, :] = halves(u_v[:, ls])
        rhs[2 * rows : 2 * rows + 16, :], rhs[2 * rows + 16 :, :] = halves(halo[...])
        out = jnp.dot(matrix[...], rhs[...], preferred_element_type=F32)
        obuf[:, ls] = out[:rows] + out[rows:]
        pltpu.make_async_copy(obuf.at[:, ls], dz.at[:, ls], sems.at[i]).start()
        return carry

    lax.fori_loop(0, chunks, step, 0)

    def finish(i, carry):
        ls = pl.ds(pl.multiple_of(i * wide, wide), wide)
        pltpu.make_async_copy(obuf.at[:, ls], dz.at[:, ls], sems.at[i]).wait()
        return carry

    lax.fori_loop(0, chunks, finish, 0)


VMEM = pl.BlockSpec(memory_space=pltpu.VMEM)
ANY = pl.BlockSpec(memory_space=pl.ANY)
PARAMS = pltpu.CompilerParams(vmem_limit_bytes=44 * 1024 * 1024)


def shards(velocity):
    rows, width = velocity.shape
    chunks = 12
    u_v, zf, zb, yf, yb = pl.pallas_call(
        functools.partial(summarize, chunks=chunks),
        out_shape=(
            pltpu.VMEM((rows, width), F32),
            jax.ShapeDtypeStruct((2, width), F32),
            jax.ShapeDtypeStruct((2, width), F32),
            jax.ShapeDtypeStruct((rows, 2 * LANES), F32),
            jax.ShapeDtypeStruct((rows, 2 * LANES), F32),
        ),
        in_specs=[ANY],
        out_specs=(VMEM,) * 5,
        scratch_shapes=[
            pltpu.VMEM((rows, BLOCK), F32),
            pltpu.VMEM((rows, BLOCK), F32),
            pltpu.SemaphoreType.DMA((chunks,)),
        ],
        compiler_params=PARAMS,
        name="summarize",
    )(velocity)

    def ring(axis, step):
        count = lax.axis_size(axis)
        return [(i, (i + step) % count) for i in range(count)]

    z_low = lax.ppermute(zf, "gz", ring("gz", 1))
    z_high = lax.ppermute(zb, "gz", ring("gz", -1))
    y_low = lax.ppermute(yf, "gy", ring("gy", 1))
    y_high = lax.ppermute(yb, "gy", ring("gy", -1))
    whole = jax.ShapeDtypeStruct((rows, width), F32)
    tall = 16
    dy = pl.pallas_call(
        functools.partial(derive_y, tall=tall),
        out_shape=whole,
        in_specs=[VMEM] * 3,
        out_specs=ANY,
        scratch_shapes=[
            pltpu.VMEM((tall, width), F32),
            pltpu.VMEM((rows, width), F32),
            pltpu.SemaphoreType.DMA((rows // tall,)),
        ],
        compiler_params=PARAMS,
        cost_estimate=pl.CostEstimate(flops=8_000_000, bytes_accessed=14_000_000, transcendentals=0),
        name="derive_y",
    )(pltpu.with_memory_space_constraint(u_v, pltpu.VMEM), y_low, y_high)
    dz = pl.pallas_call(
        functools.partial(derive_z, chunks=chunks),
        out_shape=whole,
        in_specs=[VMEM] * 4,
        out_specs=ANY,
        scratch_shapes=[
            pltpu.VMEM((2 * rows + 32, width // chunks), jnp.bfloat16),
            pltpu.VMEM((16, width // chunks), F32),
            pltpu.VMEM((rows, width), F32),
            pltpu.SemaphoreType.DMA((chunks,)),
        ],
        compiler_params=PARAMS,
        cost_estimate=pl.CostEstimate(flops=8_000_000, bytes_accessed=7_000_000, transcendentals=0),
        name="derive_z",
    )(pltpu.with_memory_space_constraint(u_v, pltpu.VMEM), z_low, z_high, jnp.asarray(z_matrix(rows)))
    return dy, dz


def solution(mesh):
    return jax.shard_map(
        shards,
        mesh=mesh,
        in_specs=(P("gz", "gy"),),
        out_specs=(P("gz", "gy"), P("gz", "gy")),
        check_vma=False,
    )
```

profile of v0, /device:TPU:1, one launch (start us, length us, event | category | flops | bytes accessed | tf_op | source)
XLA Modules:
  0.0 30.7 jit_solution(10315161390520515168)
XLA Ops:
  0.6 3.6 %summarize.1 = (f32[96,18432]{1,0:T(8,128)S(1)}, f32[2,18432]{1,0:T(2,128)S(1)}, f32[2,18432]{1,0:T(2,128)S(1)}, f32[96,256]{1,0:T(8,128)S(1)}, f32[96,256]{1,0:T(8,128)S(1)}) custom-call(f32[96,18432]{1,0:T(8,128)} %u_hbm.1), custom_call_target="tpu_custom_call" | custom-call | tf_op jit(solution)/shard_map/summarize/pallas_call | solution.py:233
  4.2 2.5 %collective-permute-start.2 = (f32[2,18432]{1,0:T(2,128)S(1)}, f32[2,18432]{1,0:T(2,128)S(1)}, u32[]{:S(2)}, u32[]{:S(2)}) collective-permute-start(f32[2,18432]{1,0:T(2,128)S(1)} %get-tuple-element.10), channel_id=1, source_target_pairs={{0,1},{1,2},{2,3},{3,4},{4,5},{5,6},{6,7},{7,8},{8,9},{9,10},{10,1... | collective-permute-start | bytes 442376 | tf_op jit(solution)/shard_map/ppermute | solution.py:257
  6.8 4.4 %collective-permute-start.3 = (f32[2,18432]{1,0:T(2,128)S(1)}, f32[2,18432]{1,0:T(2,128)S(1)}, u32[]{:S(2)}, u32[]{:S(2)}) collective-permute-start(f32[2,18432]{1,0:T(2,128)S(1)} %get-tuple-element.11), channel_id=1, source_target_pairs={{0,15},{1,0},{2,1},{3,2},{4,3},{5,4},{6,5},{7,6},{8,7},{9,8},{10,9... | collective-permute-start | bytes 442376 | tf_op jit(solution)/shard_map/ppermute | solution.py:258
  11.2 2.1 %collective-permute-start = (f32[96,256]{1,0:T(8,128)S(1)}, f32[96,256]{1,0:T(8,128)S(1)}, u32[]{:S(2)}, u32[]{:S(2)}) collective-permute-start(f32[96,256]{1,0:T(8,128)S(1)} %get-tuple-element.8), channel_id=1, source_target_pairs={{0,16},{16,32},{32,48},{48,64},{64,80},{80,96},{96,112},{112,0},{1... | collective-permute-start | bytes 294920 | tf_op jit(solution)/shard_map/ppermute | solution.py:259
  13.3 0.0 collective-permute-start.1
  13.3 1.6 %collective-permute-done.low = f32[96,256]{1,0:T(8,128)S(1)} collective-permute-done((f32[96,256]{1,0:T(8,128)S(1)}, f32[96,256]{1,0:T(8,128)S(1)}, u32[]{:S(2)}, u32[]{:S(2)}) %collective-permute-start) | collective-permute-done | bytes 98336 | tf_op jit(solution)/shard_map/ppermute | solution.py:259
  15.0 2.4 %collective-permute-done.1.high = f32[96,256]{1,0:T(8,128)S(1)} collective-permute-done((f32[96,256]{1,0:T(8,128)S(1)}, f32[96,256]{1,0:T(8,128)S(1)}, u32[]{:S(2)}, u32[]{:S(2)}) %collective-permute-start.1) | collective-permute-done | bytes 98336 | tf_op jit(solution)/shard_map/ppermute | solution.py:260
  17.4 0.0 copy-start
  17.4 8.5 %derive_y.1 = f32[96,18432]{1,0:T(8,128)} custom-call(f32[96,18432]{1,0:T(8,128)S(1)} %get-tuple-element.7.u_v, f32[96,256]{1,0:T(8,128)S(1)} %collective-permute-done.low, f32[96,256]{1,0:T(8,128)S(1)} %collective-permute-done.1.high), custom_call_target="tpu_custom_call" | custom-call | flops 8000000 | bytes 14000000 | tf_op jit(solution)/shard_map/derive_y/pallas_call | solution.py:263
  25.9 0.0 collective-permute-done.2.low
  25.9 0.0 collective-permute-done.3.high
  25.9 0.0 copy-done
  25.9 4.7 %derive_z.1 = f32[96,18432]{1,0:T(8,128)} custom-call(f32[96,18432]{1,0:T(8,128)S(1)} %get-tuple-element.7.u_v, f32[2,18432]{1,0:T(2,128)S(1)} %collective-permute-done.2.low, f32[2,18432]{1,0:T(2,128)S(1)} %collective-permute-done.3.high, bf16[192,224]{1,0:T(8,128)(2,1)S(1)} %copy-done), custom_call_target="tpu_custom_call" | custom-call | flops 8000000 | bytes 7000000 | tf_op jit(solution)/shard_map/derive_z/pallas_call | solution.py:277
Async XLA Ops:
  4.2 21.6 %collective-permute-start.2 = (f32[2,18432]{1,0:T(2,128)S(1)}, f32[2,18432]{1,0:T(2,128)S(1)}, u32[]{:S(2)}, u32[]{:S(2)}) collective-permute-start(f32[2,18432]{1,0:T(2,128)S(1)} %get-tuple-element.10), channel_id=1, source_target_pairs={{0,1},{1,2},{2,3},{3,4},{4,5},{5,6},{6,7},{7,8},{8,9},{9,10},{10,1... | collective-permute-start | bytes 442376 | tf_op jit(solution)/shard_map/ppermute | solution.py:257
  6.8 19.1 %collective-permute-start.3 = (f32[2,18432]{1,0:T(2,128)S(1)}, f32[2,18432]{1,0:T(2,128)S(1)}, u32[]{:S(2)}, u32[]{:S(2)}) collective-permute-start(f32[2,18432]{1,0:T(2,128)S(1)} %get-tuple-element.11), channel_id=1, source_target_pairs={{0,15},{1,0},{2,1},{3,2},{4,3},{5,4},{6,5},{7,6},{8,7},{9,8},{10,9... | collective-permute-start | bytes 442376 | tf_op jit(solution)/shard_map/ppermute | solution.py:258
  11.2 3.8 %collective-permute-start = (f32[96,256]{1,0:T(8,128)S(1)}, f32[96,256]{1,0:T(8,128)S(1)}, u32[]{:S(2)}, u32[]{:S(2)}) collective-permute-start(f32[96,256]{1,0:T(8,128)S(1)} %get-tuple-element.8), channel_id=1, source_target_pairs={{0,16},{16,32},{32,48},{48,64},{64,80},{80,96},{96,112},{112,0},{1... | collective-permute-start | bytes 294920 | tf_op jit(solution)/shard_map/ppermute | solution.py:259
  13.3 4.0 %collective-permute-start.1 = (f32[96,256]{1,0:T(8,128)S(1)}, f32[96,256]{1,0:T(8,128)S(1)}, u32[]{:S(2)}, u32[]{:S(2)}) collective-permute-start(f32[96,256]{1,0:T(8,128)S(1)} %get-tuple-element.9), channel_id=1, source_target_pairs={{0,112},{16,0},{32,16},{48,32},{64,48},{80,64},{96,80},{112,96},{1... | collective-permute-start | bytes 294920 | tf_op jit(solution)/shard_map/ppermute | solution.py:260
  17.4 8.6 %copy-start = (bf16[192,224]{1,0:T(8,128)(2,1)S(1)}, bf16[192,224]{1,0:T(8,128)(2,1)}, u32[]{:S(2)}) copy-start(bf16[192,224]{1,0:T(8,128)(2,1)} %constant.2.clone.matrix) | copy-start | bytes 258052
where the time goes:
time: 30.8 us; the launch traced here: 30.7 us
  Pallas kernels  16.9 us (55%)
  starting transfers between devices  9.07 us (29%)
  waiting for transfers between devices  4.04 us (13%)
  between operations  0.67 us (2%)
    pallas_call x1, Pallas kernels, shards(): pl.pallas_call(functools.partial(derive_y, tall=tall), out_shape=whole, i...  8.52 us
    pallas_call x1, Pallas kernels, shards(): pl.pallas_call(functools.partial(derive_z, chunks=chunks), out_shape=whol...  4.74 us
    ppermute x1, starting transfers between devices, shards(): z_high = lax.ppermute(zb, 'gz', ring('gz', -1))  4.4 us
    pallas_call x1, Pallas kernels, shards(): pl.pallas_call(functools.partial(summarize, chunks=chunks), out_shape=(pl...  3.61 us
    ppermute x1, starting transfers between devices, shards(): z_low = lax.ppermute(zf, 'gz', ring('gz', 1))  2.54 us
    ppermute x1, waiting for transfers between devices, shards(): y_high = lax.ppermute(yb, 'gy', ring('gy', -1))  2.4 us
    ppermute x1, starting transfers between devices, shards(): y_low = lax.ppermute(yf, 'gy', ring('gy', 1))  2.14 us
    ppermute x1, waiting for transfers between devices, shards(): y_low = lax.ppermute(yf, 'gy', ring('gy', 1))  1.64 us
  transfers between devices with their start and end apart: 4, of which 2 were waited for; matrix products, arithmetic and copies ran while one was open for 0% of the time, Pallas kernels for 28%

commit v1 on v0

v1 whole, which is shorter than its diff:
```python
import functools

import jax
import jax.numpy as jnp
import ml_dtypes
import numpy as np
from jax import lax
from jax.experimental import pallas as pl
from jax.experimental.pallas import tpu as pltpu
from jax.sharding import PartitionSpec as P

X = 96
ROOT = (5.0**0.5 - 3.0) / 2.0
EDGE = 1.0 / 12.0
GAIN = 25.0 / 12.0
LANES = 128
BLOCK = 4 * X
Q = ROOT**4
F32 = jnp.float32


def lane_index(rows):
    return lax.broadcasted_iota(jnp.int32, (rows, LANES), 1)


def rolled(x, by):
    return pltpu.roll(x, by, 1)


def is_even(axis):
    return lax.rem(lax.axis_index(axis), 2) == 0


def summarize(u_hbm, u_v, z0, z1, y0, y1, acc_f, acc_b, sems, *, chunks):
    rows, width = u_v.shape
    wide = width // chunks
    per = wide // BLOCK
    even_z, even_y = is_even("gz"), is_even("gy")

    def copy(c):
        lanes = pl.ds(c * wide, wide)
        return pltpu.make_async_copy(u_hbm.at[:, lanes], u_v.at[:, lanes], sems.at[c])

    for c in range(chunks):
        copy(c).start()
    sub = lax.broadcasted_iota(jnp.int32, (8, wide), 0)
    w_f = jnp.zeros((8, wide), F32)
    w_b = jnp.zeros((8, wide), F32)
    for r in range(8):
        w_f = jnp.where(sub == r, np.float32(ROOT ** (7 - r)), w_f)
        w_b = jnp.where(sub == r, np.float32(ROOT**r), w_b)
    for c in range(chunks):
        copy(c).wait()
        z_f = z_b = None
        for g in range(rows // 8):
            rs = slice(8 * g, 8 * g + 8)
            x = u_v[rs, c * wide : (c + 1) * wide]
            if g == 0:
                z_f, z_b = x, x
            else:
                z_f = z_f * np.float32(ROOT**8) + x
                z_b = z_b + x * np.float32(ROOT ** (8 * g))
            parts = [x[:, b * BLOCK : (b + 1) * BLOCK] for b in range(per)]
            y_f = acc_f[rs, :] if c else None
            for part in parts:
                y_f = part if y_f is None else y_f * np.float32(Q) + part
            acc_f[rs, :] = y_f
            y_b = None
            for part in reversed(parts):
                y_b = part if y_b is None else y_b * np.float32(Q) + part
            acc_b[rs, :] = acc_b[rs, :] + y_b * np.float32(Q ** (per * c)) if c else y_b
        lanes = slice(c * wide, (c + 1) * wide)
        s_f = jnp.sum(z_f * w_f, axis=0, keepdims=True)
        s_b = jnp.sum(z_b * w_b, axis=0, keepdims=True)
        e_f, e_b = u_v[rows - 1 : rows, lanes], u_v[0:1, lanes]
        z0[0:1, lanes] = jnp.where(even_z, s_f, s_b)
        z1[0:1, lanes] = jnp.where(even_z, s_b, s_f)
        z0[1:2, lanes] = jnp.where(even_z, e_f, e_b)
        z1[1:2, lanes] = jnp.where(even_z, e_b, e_f)
    lane = lane_index(8)
    for g in range(rows // 8):
        rs = slice(8 * g, 8 * g + 8)
        v0, v1, v2 = (acc_f[rs, k * LANES : (k + 1) * LANES] for k in range(3))
        s = v2 + np.float32(ROOT) * jnp.where(lane < 96, rolled(v1, 96), rolled(v2, 96))
        s = s + np.float32(ROOT**2) * jnp.where(lane < 64, rolled(v0, 64), rolled(v1, 64))
        s = s + np.float32(ROOT**3) * rolled(v0, 32)
        s_f, e_f = rolled(s, 96), rolled(u_v[rs, width - LANES :], 96)
        v0, v1, v2 = (acc_b[rs, k * LANES : (k + 1) * LANES] for k in range(3))
        s = v0 + np.float32(ROOT) * jnp.where(lane < 32, rolled(v0, 32), rolled(v1, 32))
        s = s + np.float32(ROOT**2) * jnp.where(lane < 64, rolled(v1, 64), rolled(v2, 64))
        s_b, e_b = s + np.float32(ROOT**3) * rolled(v2, 96), u_v[rs, 0:LANES]
        y0[rs, 0:LANES] = jnp.where(even_y, s_f, s_b)
        y1[rs, 0:LANES] = jnp.where(even_y, s_b, s_f)
        y0[rs, LANES:] = jnp.where(even_y, e_f, e_b)
        y1[rs, LANES:] = jnp.where(even_y, e_b, e_f)


def halves(x):
    high = x.astype(jnp.bfloat16)
    return high, (x - high.astype(F32)).astype(jnp.bfloat16)


def z_matrix(rows):
    at = np.arange(rows)
    k = at[:, None] - at[None, :]
    own = GAIN * np.sign(k) * ROOT ** np.abs(k) - EDGE * ((k == 1).astype(float) - (k == -1))
    whole = np.concatenate([own, own], axis=1).astype(np.float32)
    high = whole.astype(ml_dtypes.bfloat16)
    low = (whole - high.astype(np.float32)).astype(ml_dtypes.bfloat16)
    return np.concatenate([high, low], axis=0)


def local(u_v, matrix, z_own, v, rhs, *, chunks):
    rows, width = u_v.shape
    wide = width // chunks
    per = wide // BLOCK
    part = 48

    def step(c, carry):
        start = pl.multiple_of(c * wide, wide)
        ls = pl.ds(start, wide)
        rhs[0:rows, :], rhs[rows:, :] = halves(u_v[:, ls])
        out = jnp.dot(matrix[...], rhs[...], preferred_element_type=F32)
        z_own[:, ls] = out[:rows] + out[rows:]
        lane = lane_index(part)
        keep_low = jnp.where(c > 0, np.float32(EDGE), np.float32(0))
        keep_high = jnp.where(c < chunks - 1, np.float32(EDGE), np.float32(0))
        below = pl.multiple_of(jnp.maximum(start - LANES, 0), LANES)
        above = pl.multiple_of(jnp.minimum(start + wide, width - LANES), LANES)
        for r in range(0, rows, part):
            rs = slice(r, r + part)
            before = rolled(u_v[rs, pl.ds(below, LANES)] * keep_low, 96)
            points = []
            for b in range(per):
                at = start + b * BLOCK
                v0, v1, v2 = (
                    u_v[rs, pl.ds(pl.multiple_of(at + k * LANES, LANES), LANES)] * np.float32(EDGE) for k in range(3)
                )
                points += [
                    v0,
                    jnp.where(lane < 32, rolled(v0, 32), rolled(v1, 32)),
                    jnp.where(lane < 64, rolled(v1, 64), rolled(v2, 64)),
                    rolled(v2, 96),
                ]
            points.append(u_v[rs, pl.ds(above, LANES)] * keep_high)
            points = [before] + points
            for j in range(4 * per):
                v[4 * per * c + j, rs, :] = points[j + 2] - points[j]
        return carry

    lax.fori_loop(0, chunks, step, 0)


def finish(u_v, z_own, v, z0, z1, y0, y1, dy, dz, y, dy_v, dz_v, sem_y, sem_z, *, chunks):
    rows, width = u_v.shape
    points = v.shape[0]
    wide = width // chunks
    per = wide // BLOCK
    even_z, even_y = is_even("gz"), is_even("gy")

    def copy_z(c):
        ls = pl.ds(pl.multiple_of(c * wide, wide), wide)
        return pltpu.make_async_copy(dz_v.at[:, ls], dz.at[:, ls], sem_z.at[c])

    def copy_y(c):
        ls = pl.ds(pl.multiple_of(c * wide, wide), wide)
        return pltpu.make_async_copy(dy_v.at[:, ls], dy.at[:, ls], sem_y.at[c])

    row = lax.broadcasted_iota(jnp.int32, (8, 3 * LANES), 0)
    w_low = jnp.zeros((8, 3 * LANES), F32)
    w_high = jnp.zeros((8, 3 * LANES), F32)
    for r in range(8):
        w_low = jnp.where(row == r, np.float32(GAIN * ROOT ** (r + 1)), w_low)
        w_high = jnp.where(row == r, np.float32(-GAIN * ROOT ** (8 - r)), w_high)

    def z_step(c, carry):
        for k in range(wide // (3 * LANES)):
            ls = pl.ds(pl.multiple_of(c * wide + k * 3 * LANES, 3 * LANES), 3 * LANES)
            first, second = z0[:, ls], z1[:, ls]
            low = jnp.where(even_z, second, first)
            high = jnp.where(even_z, first, second)
            t_low, t_high = low[0:1] * w_low, high[0:1] * w_high
            for g in range(rows // 8):
                rs = slice(8 * g, 8 * g + 8)
                d = z_own[rs, ls] + t_low * np.float32(ROOT ** (8 * g))
                d = d + t_high * np.float32(ROOT ** (rows - 8 - 8 * g))
                if g == 0:
                    d = d - jnp.where(row == 0, np.float32(EDGE) * low[1:2], np.float32(0))
                if g == rows // 8 - 1:
                    d = d + jnp.where(row == 7, np.float32(EDGE) * high[1:2], np.float32(0))
                dz_v[rs, ls] = d
        copy_z(c).start()
        return carry

    lax.fori_loop(0, chunks, z_step, 0)

    tall = lane_index(rows)
    y_low = jnp.where(even_y, y1[...], y0[...]) * np.float32(EDGE)
    y_high = jnp.where(even_y, y0[...], y1[...]) * np.float32(EDGE)
    s_low, s_high = y_low[:, :LANES], y_high[:, :LANES]
    state = u_v[:, 0:LANES] * np.float32(EDGE) + s_low * np.float32(ROOT - 1 / ROOT)

    def forward(i, state):
        for k in range(4):
            state = v[4 * i + k] + state * np.float32(ROOT)
            y[4 * i + k] = state
        return state

    state = lax.fori_loop(0, points // 4, forward, state) + s_high
    y[points - 1] = state
    u_last = rolled(u_v[:, width - LANES :], 96) * np.float32(EDGE)
    after = state * np.float32(ROOT) - u_last
    far = after * np.float32(ROOT) - s_high
    state = after + far * np.float32(ROOT / (1 - ROOT * ROOT))

    def backward(i, state):
        c = chunks - 1 - i
        part = 48
        state = list(state)
        for b in reversed(range(per)):
            for h in range(rows // part):
                rs = slice(h * part, (h + 1) * part)
                d = [None] * 4
                for k in reversed(range(4)):
                    j = 4 * (per * c + b) + k
                    state[h] = y[j, rs, :] + state[h] * np.float32(ROOT)
                    d[k] = v[j, rs, :] + state[h] * np.float32(-25 * ROOT)
                lane = lane_index(part)
                d1, d2, d3 = rolled(d[1], 96), rolled(d[2], 64), rolled(d[3], 32)
                at = c * wide + b * BLOCK
                for k, o in enumerate((jnp.where(lane < 96, d[0], d1), jnp.where(lane < 64, d1, d2), jnp.where(lane < 32, d2, d3))):
                    dy_v[rs, pl.ds(pl.multiple_of(at + k * LANES, LANES), LANES)] = o

        @pl.when(i == 0)
        def _():
            edge = rolled(y_high[:, LANES:], 32)
            dy_v[:, width - LANES :] = dy_v[:, width - LANES :] + jnp.where(tall < 32, np.float32(0), edge)

        @pl.when(i == chunks - 1)
        def _():
            dy_v[:, 0:LANES] = dy_v[:, 0:LANES] - jnp.where(tall < 96, y_low[:, LANES:], np.float32(0))

        copy_y(c).start()
        return tuple(state)

    lax.fori_loop(0, chunks, backward, (state[:48], state[48:]))

    def wait(c, carry):
        copy_z(c).wait()
        copy_y(c).wait()
        return carry

    lax.fori_loop(0, chunks, wait, 0)


VMEM = pl.BlockSpec(memory_space=pltpu.VMEM)
ANY = pl.BlockSpec(memory_space=pl.ANY)


def params(mib):
    return pltpu.CompilerParams(vmem_limit_bytes=mib * 1024 * 1024)


def here(x):
    return pltpu.with_memory_space_constraint(x, pltpu.VMEM)


def shards(velocity):
    rows, width = velocity.shape
    points = width // X
    chunks = 12
    whole = jax.ShapeDtypeStruct((rows, width), F32)
    u_v, z0, z1, y0, y1 = pl.pallas_call(
        functools.partial(summarize, chunks=chunks),
        out_shape=(
            pltpu.VMEM((rows, width), F32),
            jax.ShapeDtypeStruct((2, width), F32),
            jax.ShapeDtypeStruct((2, width), F32),
            jax.ShapeDtypeStruct((rows, 2 * LANES), F32),
            jax.ShapeDtypeStruct((rows, 2 * LANES), F32),
        ),
        in_specs=[ANY],
        out_specs=(VMEM,) * 5,
        scratch_shapes=[
            pltpu.VMEM((rows, BLOCK), F32),
            pltpu.VMEM((rows, BLOCK), F32),
            pltpu.SemaphoreType.DMA((chunks,)),
        ],
        compiler_params=params(12),
        name="summarize",
    )(pltpu.with_memory_space_constraint(velocity, pltpu.HBM))

    def swap(x, axis, first):
        count = lax.axis_size(axis)
        pairs = [(i % count, (i + 1) % count) for i in range(first, count + first, 2)]
        return lax.ppermute(x, axis, pairs + [(b, a) for a, b in pairs])

    z0, z1 = swap(z0, "gz", 0), swap(z1, "gz", 1)
    y0, y1 = swap(y0, "gy", 0), swap(y1, "gy", 1)
    z_own, v = pl.pallas_call(
        functools.partial(local, chunks=chunks),
        out_shape=(pltpu.VMEM((rows, width), F32), pltpu.VMEM((points, rows, LANES), F32)),
        in_specs=[VMEM] * 2,
        out_specs=(VMEM,) * 2,
        scratch_shapes=[pltpu.VMEM((2 * rows, width // chunks), jnp.bfloat16)],
        compiler_params=params(8),
        cost_estimate=pl.CostEstimate(flops=8_000_000, bytes_accessed=10_000_000, transcendentals=0),
        name="local",
    )(here(u_v), jnp.asarray(z_matrix(rows)))
    return pl.pallas_call(
        functools.partial(finish, chunks=chunks),
        out_shape=(whole, whole),
        in_specs=[VMEM] * 7,
        out_specs=(ANY, ANY),
        scratch_shapes=[
            pltpu.VMEM((points, rows, LANES), F32),
            pltpu.VMEM((rows, width), F32),
            pltpu.VMEM((rows, width), F32),
            pltpu.SemaphoreType.DMA((chunks,)),
            pltpu.SemaphoreType.DMA((chunks,)),
        ],
        compiler_params=params(26),
        cost_estimate=pl.CostEstimate(flops=8_000_000, bytes_accessed=14_000_000, transcendentals=0),
        name="finish",
    )(here(u_v), here(z_own), here(v), z0, z1, y0, y1)


def solution(mesh):
    return jax.shard_map(
        shards,
        mesh=mesh,
        in_specs=(P("gz", "gy"),),
        out_specs=(P("gz", "gy"), P("gz", "gy")),
        check_vma=False,
    )
```

time: 30.8 us -> 25.5 us (0.83)
  the two profiles are of different devices: /device:TPU:1 before, /device:TPU:0 now
where the time goes in v1:
time: 25.5 us; the launch traced here: 25.4 us
  Pallas kernels  14.8 us (58%)
  starting transfers between devices  9.93 us (39%)
  between operations  0.69 us (3%)
    ppermute x4, starting transfers between devices, swap(): return lax.ppermute(x, axis, pairs + [(b, a) for a, b in pairs])  9.93 us
    pallas_call x1, Pallas kernels, shards(): pl.pallas_call(functools.partial(finish, chunks=chunks), out_shape=(whole...  6.66 us
    pallas_call x1, Pallas kernels, shards(): pl.pallas_call(functools.partial(local, chunks=chunks), out_shape=(pltpu....  4.53 us
    pallas_call x1, Pallas kernels, shards(): pl.pallas_call(functools.partial(summarize, chunks=chunks), out_shape=(pl...  3.6 us
  transfers between devices with their start and end apart: 4, of which 0 were waited for; matrix products, arithmetic and copies ran while one was open for 0% of the time, Pallas kernels for 18%

profile of v1, /device:TPU:0, one launch (start us, length us, event | category | flops | bytes accessed | tf_op | source)
XLA Modules:
  0.0 25.4 jit_solution(13734341267967411725)
XLA Ops:
  0.6 0.0 copy-start
  0.6 3.6 %summarize.1 = (f32[96,18432]{1,0:T(8,128)S(1)}, f32[2,18432]{1,0:T(2,128)S(1)}, f32[2,18432]{1,0:T(2,128)S(1)}, f32[96,256]{1,0:T(8,128)S(1)}, f32[96,256]{1,0:T(8,128)S(1)}) custom-call(f32[96,18432]{1,0:T(8,128)} %u_hbm.1), custom_call_target="tpu_custom_call" | custom-call | tf_op jit(solution)/shard_map/summarize/pallas_call | solution.py:273
  4.2 2.1 %collective-permute-start = (f32[2,18432]{1,0:T(2,128)S(1)}, f32[2,18432]{1,0:T(2,128)S(1)}, u32[]{:S(2)}, u32[]{:S(2)}) collective-permute-start(f32[2,18432]{1,0:T(2,128)S(1)} %get-tuple-element.12), channel_id=1, source_target_pairs={{0,1},{2,3},{4,5},{6,7},{8,9},{10,11},{12,13},{14,15},{1,0},{3,2},... | collective-permute-start | bytes 442376 | tf_op jit(solution)/shard_map/ppermute | solution.py:296
  6.3 4.7 %collective-permute-start.1 = (f32[2,18432]{1,0:T(2,128)S(1)}, f32[2,18432]{1,0:T(2,128)S(1)}, u32[]{:S(2)}, u32[]{:S(2)}) collective-permute-start(f32[2,18432]{1,0:T(2,128)S(1)} %get-tuple-element.13), channel_id=1, source_target_pairs={{1,2},{3,4},{5,6},{7,8},{9,10},{11,12},{13,14},{15,0},{2,1},{4,3},... | collective-permute-start | bytes 442376 | tf_op jit(solution)/shard_map/ppermute | solution.py:296
  11.0 0.0 collective-permute-start.2
  11.0 3.1 %collective-permute-start.3 = (f32[96,256]{1,0:T(8,128)S(1)}, f32[96,256]{1,0:T(8,128)S(1)}, u32[]{:S(2)}, u32[]{:S(2)}) collective-permute-start(f32[96,256]{1,0:T(8,128)S(1)} %get-tuple-element.15), channel_id=1, source_target_pairs={{16,32},{48,64},{80,96},{112,0},{32,16},{64,48},{96,80},{0,112},{1... | collective-permute-start | bytes 294920 | tf_op jit(solution)/shard_map/ppermute | solution.py:296
  14.2 0.0 copy-done
  14.2 4.5 %local.1 = (f32[96,18432]{1,0:T(8,128)S(1)}, f32[192,96,128]{2,1,0:T(8,128)S(1)}) custom-call(f32[96,18432]{1,0:T(8,128)S(1)} %get-tuple-element.9.u_v, bf16[192,192]{1,0:T(8,128)(2,1)S(1)} %copy-done), custom_call_target="tpu_custom_call" | custom-call | flops 8000000 | bytes 10000000 | tf_op jit(solution)/shard_map/local/pallas_call | solution.py:300
  18.7 0.0 collective-permute-done.2.y0
  18.7 0.0 collective-permute-done.3.y1
  18.7 0.0 collective-permute-done.z0
  18.8 0.0 collective-permute-done.1.z1
  18.8 6.7 %finish.1 = (f32[96,18432]{1,0:T(8,128)}, f32[96,18432]{1,0:T(8,128)}) custom-call(f32[96,18432]{1,0:T(8,128)S(1)} %get-tuple-element.9.u_v, f32[96,18432]{1,0:T(8,128)S(1)} %get-tuple-element.10.z_own, f32[192,96,128]{2,1,0:T(8,128)S(1)} %get-tuple-element.11.v, f32[2,18432]{1,0:T(2,128)S(1)} %collective-permute-done.z0, ...), custom_call_target="tpu_custom_call" | custom-call | flops 8000000 | bytes 14000000 | tf_op jit(solution)/shard_map/finish/pallas_call | solution.py:310
Async XLA Ops:
  0.6 13.6 %copy-start = (bf16[192,192]{1,0:T(8,128)(2,1)S(1)}, bf16[192,192]{1,0:T(8,128)(2,1)}, u32[]{:S(2)}) copy-start(bf16[192,192]{1,0:T(8,128)(2,1)} %constant.2.clone.matrix) | copy-start | bytes 221188
  4.2 14.5 %collective-permute-start = (f32[2,18432]{1,0:T(2,128)S(1)}, f32[2,18432]{1,0:T(2,128)S(1)}, u32[]{:S(2)}, u32[]{:S(2)}) collective-permute-start(f32[2,18432]{1,0:T(2,128)S(1)} %get-tuple-element.12), channel_id=1, source_target_pairs={{0,1},{2,3},{4,5},{6,7},{8,9},{10,11},{12,13},{14,15},{1,0},{3,2},... | collective-permute-start | bytes 442376 | tf_op jit(solution)/shard_map/ppermute | solution.py:296
  6.3 12.4 %collective-permute-start.1 = (f32[2,18432]{1,0:T(2,128)S(1)}, f32[2,18432]{1,0:T(2,128)S(1)}, u32[]{:S(2)}, u32[]{:S(2)}) collective-permute-start(f32[2,18432]{1,0:T(2,128)S(1)} %get-tuple-element.13), channel_id=1, source_target_pairs={{1,2},{3,4},{5,6},{7,8},{9,10},{11,12},{13,14},{15,0},{2,1},{4,3},... | collective-permute-start | bytes 442376 | tf_op jit(solution)/shard_map/ppermute | solution.py:296
  11.0 7.7 %collective-permute-start.2 = (f32[96,256]{1,0:T(8,128)S(1)}, f32[96,256]{1,0:T(8,128)S(1)}, u32[]{:S(2)}, u32[]{:S(2)}) collective-permute-start(f32[96,256]{1,0:T(8,128)S(1)} %get-tuple-element.14), channel_id=1, source_target_pairs={{0,16},{32,48},{64,80},{96,112},{16,0},{48,32},{80,64},{112,96},{1... | collective-permute-start | bytes 294920 | tf_op jit(solution)/shard_map/ppermute | solution.py:296
  11.0 7.7 %collective-permute-start.3 = (f32[96,256]{1,0:T(8,128)S(1)}, f32[96,256]{1,0:T(8,128)S(1)}, u32[]{:S(2)}, u32[]{:S(2)}) collective-permute-start(f32[96,256]{1,0:T(8,128)S(1)} %get-tuple-element.15), channel_id=1, source_target_pairs={{16,32},{48,64},{80,96},{112,0},{32,16},{64,48},{96,80},{0,112},{1... | collective-permute-start | bytes 294920 | tf_op jit(solution)/shard_map/ppermute | solution.py:296

commit v2 on v1

--- a/solution.py
+++ b/solution.py
@@ -16,6 +16,9 @@
 LANES = 128
 BLOCK = 4 * X
 Q = ROOT**4
+UL = 2
+UF = 4
+FORWARD = 48
 F32 = jnp.float32
 
 
@@ -110,113 +113,108 @@
     return np.concatenate([high, low], axis=0)
 
 
-def local(u_v, matrix, z_own, v, rhs, *, chunks):
+def local(u_v, matrix, z_own, v, rhs, last, *, chunks, unroll):
     rows, width = u_v.shape
     wide = width // chunks
     per = wide // BLOCK
-    part = 48
-
-    def step(c, carry):
-        start = pl.multiple_of(c * wide, wide)
-        ls = pl.ds(start, wide)
-        rhs[0:rows, :], rhs[rows:, :] = halves(u_v[:, ls])
-        out = jnp.dot(matrix[...], rhs[...], preferred_element_type=F32)
+    part = rows // 4
+    lane = lane_index(part)
+    last[...] = jnp.zeros((rows, LANES), F32)
+
+    for c in range(chunks):
+        ls = slice(c * wide, (c + 1) * wide)
+        slot = c % unroll
+        rhs[slot, 0:rows, :], rhs[slot, rows:, :] = halves(u_v[:, ls])
+        out = jnp.dot(matrix[...], rhs[slot], preferred_element_type=F32)
         z_own[:, ls] = out[:rows] + out[rows:]
-        lane = lane_index(part)
-        keep_low = jnp.where(c > 0, np.float32(EDGE), np.float32(0))
-        keep_high = jnp.where(c < chunks - 1, np.float32(EDGE), np.float32(0))
-        below = pl.multiple_of(jnp.maximum(start - LANES, 0), LANES)
-        above = pl.multiple_of(jnp.minimum(start + wide, width - LANES), LANES)
         for r in range(0, rows, part):
             rs = slice(r, r + part)
-            before = rolled(u_v[rs, pl.ds(below, LANES)] * keep_low, 96)
-            points = []
+            points = [last[rs, :]]
             for b in range(per):
-                at = start + b * BLOCK
-                v0, v1, v2 = (
-                    u_v[rs, pl.ds(pl.multiple_of(at + k * LANES, LANES), LANES)] * np.float32(EDGE) for k in range(3)
-                )
+                at = c * wide + b * BLOCK
+                v0, v1, v2 = (u_v[rs, at + k * LANES : at + (k + 1) * LANES] * np.float32(EDGE) for k in range(3))
                 points += [
                     v0,
-                    jnp.where(lane < 32, rolled(v0, 32), rolled(v1, 32)),
-                    jnp.where(lane < 64, rolled(v1, 64), rolled(v2, 64)),
+                    rolled(jnp.where(lane < 96, v1, v0), 32),
+                    rolled(jnp.where(lane < 64, v2, v1), 64),
                     rolled(v2, 96),
                 ]
-            points.append(u_v[rs, pl.ds(above, LANES)] * keep_high)
-            points = [before] + points
-            for j in range(4 * per):
-                v[4 * per * c + j, rs, :] = points[j + 2] - points[j]
-        return carry
-
-    lax.fori_loop(0, chunks, step, 0)
-
-
-def finish(u_v, z_own, v, z0, z1, y0, y1, dy, dz, y, dy_v, dz_v, sem_y, sem_z, *, chunks):
+            last[rs, :] = points[-1]
+            if c < chunks - 1:
+                points.append(u_v[rs, (c + 1) * wide : (c + 1) * wide + LANES] * np.float32(EDGE))
+            else:
+                points.append(jnp.zeros((part, LANES), F32))
+            for k in range(4 * per):
+                v[4 * per * c + k, rs, :] = points[k + 2] - points[k]
+
+
+def halo_matrix(rows):
+    at = np.arange(rows)
+    whole = np.zeros((rows, 8))
+    whole[:, 0] = GAIN * ROOT ** (at + 1.0)
+    whole[0, 1] = -EDGE
+    whole[:, 2] = -GAIN * ROOT ** (rows - at * 1.0)
+    whole[rows - 1, 3] = EDGE
+    whole = whole.astype(np.float32)
+    high = whole.astype(ml_dtypes.bfloat16)
+    low = (whole - high.astype(np.float32)).astype(ml_dtypes.bfloat16)
+    return np.concatenate([high, high, low, low], axis=1)
+
+
+def finish(u_v, z_own, v, matrix, z0, z1, y0, y1, dy, dz, y, dy_v, dz_v, halo, rhs, sem_y, sem_z, *, chunks, unroll):
     rows, width = u_v.shape
     points = v.shape[0]
     wide = width // chunks
     per = wide // BLOCK
     even_z, even_y = is_even("gz"), is_even("gy")
 
-    def copy_z(c):
+    def copy(buffer, out, sems, c):
         ls = pl.ds(pl.multiple_of(c * wide, wide), wide)
-        return pltpu.make_async_copy(dz_v.at[:, ls], dz.at[:, ls], sem_z.at[c])
-
-    def copy_y(c):
-        ls = pl.ds(pl.multiple_of(c * wide, wide), wide)
-        return pltpu.make_async_copy(dy_v.at[:, ls], dy.at[:, ls], sem_y.at[c])
-
-    row = lax.broadcasted_iota(jnp.int32, (8, 3 * LANES), 0)
-    w_low = jnp.zeros((8, 3 * LANES), F32)
-    w_high = jnp.zeros((8, 3 * LANES), F32)
-    for r in range(8):
-        w_low = jnp.where(row == r, np.float32(GAIN * ROOT ** (r + 1)), w_low)
-        w_high = jnp.where(row == r, np.float32(-GAIN * ROOT ** (8 - r)), w_high)
-
-    def z_step(c, carry):
-        for k in range(wide // (3 * LANES)):
-            ls = pl.ds(pl.multiple_of(c * wide + k * 3 * LANES, 3 * LANES), 3 * LANES)
+        return pltpu.make_async_copy(buffer.at[:, ls], out.at[:, ls], sems.at[c])
+
+    halo[...] = jnp.zeros(halo.shape, F32)
+
+    def z_step(i, carry):
+        for s in range(unroll):
+            c = i * unroll + s
+            slot = s
+            ls = pl.ds(pl.multiple_of(c * wide, wide), wide)
             first, second = z0[:, ls], z1[:, ls]
-            low = jnp.where(even_z, second, first)
-            high = jnp.where(even_z, first, second)
-            t_low, t_high = low[0:1] * w_low, high[0:1] * w_high
-            for g in range(rows // 8):
-                rs = slice(8 * g, 8 * g + 8)
-                d = z_own[rs, ls] + t_low * np.float32(ROOT ** (8 * g))
-                d = d + t_high * np.float32(ROOT ** (rows - 8 - 8 * g))
-                if g == 0:
-                    d = d - jnp.where(row == 0, np.float32(EDGE) * low[1:2], np.float32(0))
-                if g == rows // 8 - 1:
-                    d = d + jnp.where(row == 7, np.float32(EDGE) * high[1:2], np.float32(0))
-                dz_v[rs, ls] = d
-        copy_z(c).start()
+            halo[slot, 0:2, :] = jnp.where(even_z, second, first)
+            halo[slot, 2:4, :] = jnp.where(even_z, first, second)
+            h = halo[slot]
+            high = h.astype(jnp.bfloat16).astype(F32)
+            both = jnp.concatenate([high, h - high], axis=0).astype(jnp.bfloat16)
+            rhs[slot, 0:16, :] = both
+            rhs[slot, 16:32, :] = both
+            dz_v[:, ls] = z_own[:, ls] + jnp.dot(matrix[...], rhs[slot], preferred_element_type=F32)
+            copy(dz_v, dz, sem_z, c).start()
         return carry
 
-    lax.fori_loop(0, chunks, z_step, 0)
-
-    tall = lane_index(rows)
+    lax.fori_loop(0, chunks // unroll, z_step, 0)
+
     y_low = jnp.where(even_y, y1[...], y0[...]) * np.float32(EDGE)
     y_high = jnp.where(even_y, y0[...], y1[...]) * np.float32(EDGE)
     s_low, s_high = y_low[:, :LANES], y_high[:, :LANES]
     state = u_v[:, 0:LANES] * np.float32(EDGE) + s_low * np.float32(ROOT - 1 / ROOT)
 
     def forward(i, state):
-        for k in range(4):
-            state = v[4 * i + k] + state * np.float32(ROOT)
-            y[4 * i + k] = state
+        for k in range(FORWARD):
+            j = FORWARD * i + k
+            state = v[j] + state * np.float32(ROOT)
+            y[j] = state
         return state
 
-    state = lax.fori_loop(0, points // 4, forward, state) + s_high
+    state = lax.fori_loop(0, points // FORWARD, forward, state) + s_high
     y[points - 1] = state
     u_last = rolled(u_v[:, width - LANES :], 96) * np.float32(EDGE)
     after = state * np.float32(ROOT) - u_last
     far = after * np.float32(ROOT) - s_high
     state = after + far * np.float32(ROOT / (1 - ROOT * ROOT))
-
-    def backward(i, state):
-        c = chunks - 1 - i
-        part = 48
-        state = list(state)
+    part = rows // 2
+    lane = lane_index(part)
+    state = [state[:part], state[part:]]
+    for c in reversed(range(chunks)):
         for b in reversed(range(per)):
             for h in range(rows // part):
                 rs = slice(h * part, (h + 1) * part)
@@ -225,32 +223,19 @@
                     j = 4 * (per * c + b) + k
                     state[h] = y[j, rs, :] + state[h] * np.float32(ROOT)
                     d[k] = v[j, rs, :] + state[h] * np.float32(-25 * ROOT)
-                lane = lane_index(part)
+                    if j == points - 1:
+                        d[k] = d[k] + y_high[rs, LANES:]
+                    if j == 0:
+                        d[k] = d[k] - y_low[rs, LANES:]
                 d1, d2, d3 = rolled(d[1], 96), rolled(d[2], 64), rolled(d[3], 32)
                 at = c * wide + b * BLOCK
                 for k, o in enumerate((jnp.where(lane < 96, d[0], d1), jnp.where(lane < 64, d1, d2), jnp.where(lane < 32, d2, d3))):
-                    dy_v[rs, pl.ds(pl.multiple_of(at + k * LANES, LANES), LANES)] = o
-
-        @pl.when(i == 0)
-        def _():
-            edge = rolled(y_high[:, LANES:], 32)
-            dy_v[:, width - LANES :] = dy_v[:, width - LANES :] + jnp.where(tall < 32, np.float32(0), edge)
-
-        @pl.when(i == chunks - 1)
-        def _():
-            dy_v[:, 0:LANES] = dy_v[:, 0:LANES] - jnp.where(tall < 96, y_low[:, LANES:], np.float32(0))
-
-        copy_y(c).start()
-        return tuple(state)
-
-    lax.fori_loop(0, chunks, backward, (state[:48], state[48:]))
-
-    def wait(c, carry):
-        copy_z(c).wait()
-        copy_y(c).wait()
-        return carry
-
-    lax.fori_loop(0, chunks, wait, 0)
+                    dy_v[rs, at + k * LANES : at + (k + 1) * LANES] = o
+        copy(dy_v, dy, sem_y, c).start()
+
+    for c in range(chunks):
+        copy(dz_v, dz, sem_z, c).wait()
+        copy(dy_v, dy, sem_y, c).wait()
 
 
 VMEM = pl.BlockSpec(memory_space=pltpu.VMEM)
@@ -295,34 +280,37 @@
         pairs = [(i % count, (i + 1) % count) for i in range(first, count + first, 2)]
         return lax.ppermute(x, axis, pairs + [(b, a) for a, b in pairs])
 
-    z0, z1 = swap(z0, "gz", 0), swap(z1, "gz", 1)
+    z1 = swap(z1, "gz", 1)
+    z0 = swap(z0, "gz", 0)
     y0, y1 = swap(y0, "gy", 0), swap(y1, "gy", 1)
     z_own, v = pl.pallas_call(
-        functools.partial(local, chunks=chunks),
+        functools.partial(local, chunks=chunks, unroll=UL),
         out_shape=(pltpu.VMEM((rows, width), F32), pltpu.VMEM((points, rows, LANES), F32)),
         in_specs=[VMEM] * 2,
         out_specs=(VMEM,) * 2,
-        scratch_shapes=[pltpu.VMEM((2 * rows, width // chunks), jnp.bfloat16)],
+        scratch_shapes=[pltpu.VMEM((UL, 2 * rows, width // chunks), jnp.bfloat16), pltpu.VMEM((rows, LANES), F32)],
         compiler_params=params(8),
         cost_estimate=pl.CostEstimate(flops=8_000_000, bytes_accessed=10_000_000, transcendentals=0),
         name="local",
     )(here(u_v), jnp.asarray(z_matrix(rows)))
     return pl.pallas_call(
-        functools.partial(finish, chunks=chunks),
+        functools.partial(finish, chunks=chunks, unroll=UF),
         out_shape=(whole, whole),
-        in_specs=[VMEM] * 7,
+        in_specs=[VMEM] * 8,
         out_specs=(ANY, ANY),
         scratch_shapes=[
             pltpu.VMEM((points, rows, LANES), F32),
             pltpu.VMEM((rows, width), F32),
             pltpu.VMEM((rows, width), F32),
+            pltpu.VMEM((UF, 8, width // chunks), F32),
+            pltpu.VMEM((UF, 32, width // chunks), jnp.bfloat16),
             pltpu.SemaphoreType.DMA((chunks,)),
             pltpu.SemaphoreType.DMA((chunks,)),
         ],
         compiler_params=params(26),
         cost_estimate=pl.CostEstimate(flops=8_000_000, bytes_accessed=14_000_000, transcendentals=0),
         name="finish",
-    )(here(u_v), here(z_own), here(v), z0, z1, y0, y1)
+    )(here(u_v), here(z_own), here(v), jnp.asarray(halo_matrix(rows)), z0, z1, y0, y1)
 
 
 def solution(mesh):

time: 25.5 us -> 22.8 us (0.89)
  Pallas kernels: 14.8 us -> 12 us
    pallas_call x2, Pallas kernels: 11.2 us -> 8.31 us  [the longest x1 5.55 us: shards(): pl.pallas_call(functools.partial(finish, chunks=chunks, unroll=UF), out_s...]
  transfers between devices with their start and end apart: 4 -> 4, of which waited for: 0 -> 0; matrix products, arithmetic and copies ran while one was open for 0% -> 0% of each run, Pallas kernels for 18% -> 12%
where the time goes in v2:
time: 22.8 us; the launch traced here: 22.7 us
  Pallas kernels  12 us (53%)
  starting transfers between devices  9.93 us (44%)
  between operations  0.7 us (3%)
    ppermute x4, starting transfers between devices, swap(): return lax.ppermute(x, axis, pairs + [(b, a) for a, b in pairs])  9.93 us
    pallas_call x1, Pallas kernels, shards(): pl.pallas_call(functools.partial(finish, chunks=chunks, unroll=UF), out_s...  5.55 us
    pallas_call x1, Pallas kernels, shards(): pl.pallas_call(functools.partial(summarize, chunks=chunks), out_shape=(pl...  3.71 us
    pallas_call x1, Pallas kernels, shards(): pl.pallas_call(functools.partial(local, chunks=chunks, unroll=UL), out_sh...  2.76 us
  transfers between devices with their start and end apart: 4, of which 0 were waited for; matrix products, arithmetic and copies ran while one was open for 0% of the time, Pallas kernels for 12%

profile of v2, /device:TPU:0, one launch (start us, length us, event | category | flops | bytes accessed | tf_op | source)
XLA Modules:
  0.0 22.7 jit_solution(3299686534570664292)
XLA Ops:
  0.6 0.0 copy-start
  0.6 0.0 copy-start.1
  0.7 3.7 %summarize.1 = (f32[96,18432]{1,0:T(8,128)S(1)}, f32[2,18432]{1,0:T(2,128)S(1)}, f32[2,18432]{1,0:T(2,128)S(1)}, f32[96,256]{1,0:T(8,128)S(1)}, f32[96,256]{1,0:T(8,128)S(1)}) custom-call(f32[96,18432]{1,0:T(8,128)} %u_hbm.1), custom_call_target="tpu_custom_call" | custom-call | tf_op jit(solution)/shard_map/summarize/pallas_call | solution.py:258
  4.4 2.1 %collective-permute-start = (f32[2,18432]{1,0:T(2,128)S(1)}, f32[2,18432]{1,0:T(2,128)S(1)}, u32[]{:S(2)}, u32[]{:S(2)}) collective-permute-start(f32[2,18432]{1,0:T(2,128)S(1)} %get-tuple-element.12), channel_id=1, source_target_pairs={{0,1},{2,3},{4,5},{6,7},{8,9},{10,11},{12,13},{14,15},{1,0},{3,2},... | collective-permute-start | bytes 442376 | tf_op jit(solution)/shard_map/ppermute | solution.py:281
  6.4 4.7 %collective-permute-start.1 = (f32[2,18432]{1,0:T(2,128)S(1)}, f32[2,18432]{1,0:T(2,128)S(1)}, u32[]{:S(2)}, u32[]{:S(2)}) collective-permute-start(f32[2,18432]{1,0:T(2,128)S(1)} %get-tuple-element.13), channel_id=1, source_target_pairs={{1,2},{3,4},{5,6},{7,8},{9,10},{11,12},{13,14},{15,0},{2,1},{4,3},... | collective-permute-start | bytes 442376 | tf_op jit(solution)/shard_map/ppermute | solution.py:281
  11.2 0.0 collective-permute-start.2
  11.2 3.1 %collective-permute-start.3 = (f32[96,256]{1,0:T(8,128)S(1)}, f32[96,256]{1,0:T(8,128)S(1)}, u32[]{:S(2)}, u32[]{:S(2)}) collective-permute-start(f32[96,256]{1,0:T(8,128)S(1)} %get-tuple-element.15), channel_id=1, source_target_pairs={{16,32},{48,64},{80,96},{112,0},{32,16},{64,48},{96,80},{0,112},{1... | collective-permute-start | bytes 294920 | tf_op jit(solution)/shard_map/ppermute | solution.py:281
  14.3 0.0 copy-done
  14.3 2.8 %local.1 = (f32[96,18432]{1,0:T(8,128)S(1)}, f32[192,96,128]{2,1,0:T(8,128)S(1)}) custom-call(f32[96,18432]{1,0:T(8,128)S(1)} %get-tuple-element.9.u_v, bf16[192,192]{1,0:T(8,128)(2,1)S(1)} %copy-done), custom_call_target="tpu_custom_call" | custom-call | flops 8000000 | bytes 10000000 | tf_op jit(solution)/shard_map/local/pallas_call | solution.py:286
  17.1 0.0 collective-permute-done.2.y0
  17.1 0.0 collective-permute-done.3.y1
  17.1 0.0 collective-permute-done.z0
  17.1 0.0 collective-permute-done.1.z1
  17.1 0.0 copy-done.1
  17.1 5.5 %finish.1 = (f32[96,18432]{1,0:T(8,128)}, f32[96,18432]{1,0:T(8,128)}) custom-call(f32[96,18432]{1,0:T(8,128)S(1)} %get-tuple-element.9.u_v, f32[96,18432]{1,0:T(8,128)S(1)} %get-tuple-element.10.z_own, f32[192,96,128]{2,1,0:T(8,128)S(1)} %get-tuple-element.11.v, bf16[96,32]{1,0:T(8,128)(2,1)S(1)} %copy-done.1, f32[2,18432]{1,0:T(2,128)S(1)} %collective-permute-done.z0, ...), custom_call_target="tpu_custom_call" | custom-call | flops 8000000 | bytes 14000000 | tf_op jit(solution)/shard_map/finish/pallas_call | solution.py:296
Async XLA Ops:
  0.6 13.7 %copy-start = (bf16[192,192]{1,0:T(8,128)(2,1)S(1)}, bf16[192,192]{1,0:T(8,128)(2,1)}, u32[]{:S(2)}) copy-start(bf16[192,192]{1,0:T(8,128)(2,1)} %constant.4.clone.matrix) | copy-start | bytes 221188
  0.6 16.5 %copy-start.1 = (bf16[96,32]{1,0:T(8,128)(2,1)S(1)}, bf16[96,32]{1,0:T(8,128)(2,1)}, u32[]{:S(2)}) copy-start(bf16[96,32]{1,0:T(8,128)(2,1)} %constant.5.clone.matrix) | copy-start | bytes 18436
  4.4 12.7 %collective-permute-start = (f32[2,18432]{1,0:T(2,128)S(1)}, f32[2,18432]{1,0:T(2,128)S(1)}, u32[]{:S(2)}, u32[]{:S(2)}) collective-permute-start(f32[2,18432]{1,0:T(2,128)S(1)} %get-tuple-element.12), channel_id=1, source_target_pairs={{0,1},{2,3},{4,5},{6,7},{8,9},{10,11},{12,13},{14,15},{1,0},{3,2},... | collective-permute-start | bytes 442376 | tf_op jit(solution)/shard_map/ppermute | solution.py:281
  6.4 10.7 %collective-permute-start.1 = (f32[2,18432]{1,0:T(2,128)S(1)}, f32[2,18432]{1,0:T(2,128)S(1)}, u32[]{:S(2)}, u32[]{:S(2)}) collective-permute-start(f32[2,18432]{1,0:T(2,128)S(1)} %get-tuple-element.13), channel_id=1, source_target_pairs={{1,2},{3,4},{5,6},{7,8},{9,10},{11,12},{13,14},{15,0},{2,1},{4,3},... | collective-permute-start | bytes 442376 | tf_op jit(solution)/shard_map/ppermute | solution.py:281
  11.2 5.9 %collective-permute-start.2 = (f32[96,256]{1,0:T(8,128)S(1)}, f32[96,256]{1,0:T(8,128)S(1)}, u32[]{:S(2)}, u32[]{:S(2)}) collective-permute-start(f32[96,256]{1,0:T(8,128)S(1)} %get-tuple-element.14), channel_id=1, source_target_pairs={{0,16},{32,48},{64,80},{96,112},{16,0},{48,32},{80,64},{112,96},{1... | collective-permute-start | bytes 294920 | tf_op jit(solution)/shard_map/ppermute | solution.py:281
  11.2 5.9 %collective-permute-start.3 = (f32[96,256]{1,0:T(8,128)S(1)}, f32[96,256]{1,0:T(8,128)S(1)}, u32[]{:S(2)}, u32[]{:S(2)}) collective-permute-start(f32[96,256]{1,0:T(8,128)S(1)} %get-tuple-element.15), channel_id=1, source_target_pairs={{16,32},{48,64},{80,96},{112,0},{32,16},{64,48},{96,80},{0,112},{1... | collective-permute-start | bytes 294920 | tf_op jit(solution)/shard_map/ppermute | solution.py:281

commit v3 on v2

--- a/solution.py
+++ b/solution.py
@@ -34,7 +34,7 @@
     return lax.rem(lax.axis_index(axis), 2) == 0
 
 
-def summarize(u_hbm, u_v, z0, z1, y0, y1, acc_f, acc_b, sems, *, chunks):
+def summarize(u_hbm, m_hbm, u_v, z0, z1, y0, y1, z_own, v, acc_f, acc_b, matrix, rhs, last, sems, *, chunks, unroll):
     rows, width = u_v.shape
     wide = width // chunks
     per = wide // BLOCK
@@ -46,6 +46,8 @@
 
     for c in range(chunks):
         copy(c).start()
+    fetch = pltpu.make_async_copy(m_hbm, matrix, sems.at[chunks])
+    fetch.start()
     sub = lax.broadcasted_iota(jnp.int32, (8, wide), 0)
     w_f = jnp.zeros((8, wide), F32)
     w_b = jnp.zeros((8, wide), F32)
@@ -81,6 +83,7 @@
         z0[1:2, lanes] = jnp.where(even_z, e_f, e_b)
         z1[1:2, lanes] = jnp.where(even_z, e_b, e_f)
     lane = lane_index(8)
+    y1[rows:, :] = jnp.zeros((8, 2 * LANES), F32)
     for g in range(rows // 8):
         rs = slice(8 * g, 8 * g + 8)
         v0, v1, v2 = (acc_f[rs, k * LANES : (k + 1) * LANES] for k in range(3))
@@ -96,6 +99,11 @@
         y1[rs, 0:LANES] = jnp.where(even_y, s_b, s_f)
         y0[rs, LANES:] = jnp.where(even_y, e_f, e_b)
         y1[rs, LANES:] = jnp.where(even_y, e_b, e_f)
+    fetch.wait()
+
+    @pl.when(at_wrap())
+    def _():
+        own_parts(u_v, matrix, z_own, v, rhs, last, chunks=chunks, unroll=unroll)
 
 
 def halves(x):
@@ -113,7 +121,7 @@
     return np.concatenate([high, low], axis=0)
 
 
-def local(u_v, matrix, z_own, v, rhs, last, *, chunks, unroll):
+def own_parts(u_v, matrix, z_own, v, rhs, last, *, chunks, unroll):
     rows, width = u_v.shape
     wide = width // chunks
     per = wide // BLOCK
@@ -148,6 +156,18 @@
                 v[4 * per * c + k, rs, :] = points[k + 2] - points[k]
 
 
+def at_wrap():
+    return lax.axis_index("gz") == 0
+
+
+def local(u_v, matrix, z_before, v_before, z_own, v, rhs, last, *, chunks, unroll):
+    del z_before, v_before
+
+    @pl.when(jnp.logical_not(at_wrap()))
+    def _():
+        own_parts(u_v, matrix, z_own, v, rhs, last, chunks=chunks, unroll=unroll)
+
+
 def halo_matrix(rows):
     at = np.arange(rows)
     whole = np.zeros((rows, 8))
@@ -193,8 +213,8 @@
 
     lax.fori_loop(0, chunks // unroll, z_step, 0)
 
-    y_low = jnp.where(even_y, y1[...], y0[...]) * np.float32(EDGE)
-    y_high = jnp.where(even_y, y0[...], y1[...]) * np.float32(EDGE)
+    y_low = jnp.where(even_y, y1[0:rows, :], y0[...]) * np.float32(EDGE)
+    y_high = jnp.where(even_y, y0[...], y1[0:rows, :]) * np.float32(EDGE)
     s_low, s_high = y_low[:, :LANES], y_high[:, :LANES]
     state = u_v[:, 0:LANES] * np.float32(EDGE) + s_low * np.float32(ROOT - 1 / ROOT)
 
@@ -255,25 +275,31 @@
     points = width // X
     chunks = 12
     whole = jax.ShapeDtypeStruct((rows, width), F32)
-    u_v, z0, z1, y0, y1 = pl.pallas_call(
-        functools.partial(summarize, chunks=chunks),
+    matrix = jnp.asarray(z_matrix(rows))
+    u_v, z0, z1, y0, y1, z_own, v = pl.pallas_call(
+        functools.partial(summarize, chunks=chunks, unroll=UL),
         out_shape=(
             pltpu.VMEM((rows, width), F32),
             jax.ShapeDtypeStruct((2, width), F32),
             jax.ShapeDtypeStruct((2, width), F32),
             jax.ShapeDtypeStruct((rows, 2 * LANES), F32),
-            jax.ShapeDtypeStruct((rows, 2 * LANES), F32),
+            jax.ShapeDtypeStruct((rows + 8, 2 * LANES), F32),
+            pltpu.VMEM((rows, width), F32),
+            pltpu.VMEM((points, rows, LANES), F32),
         ),
-        in_specs=[ANY],
-        out_specs=(VMEM,) * 5,
+        in_specs=[ANY] * 2,
+        out_specs=(VMEM,) * 7,
         scratch_shapes=[
             pltpu.VMEM((rows, BLOCK), F32),
             pltpu.VMEM((rows, BLOCK), F32),
-            pltpu.SemaphoreType.DMA((chunks,)),
+            pltpu.VMEM((2 * rows, 2 * rows), jnp.bfloat16),
+            pltpu.VMEM((UL, 2 * rows, width // chunks), jnp.bfloat16),
+            pltpu.VMEM((rows, LANES), F32),
+            pltpu.SemaphoreType.DMA((chunks + 1,)),
         ],
         compiler_params=params(12),
         name="summarize",
-    )(pltpu.with_memory_space_constraint(velocity, pltpu.HBM))
+    )(pltpu.with_memory_space_constraint(velocity, pltpu.HBM), pltpu.with_memory_space_constraint(matrix, pltpu.HBM))
 
     def swap(x, axis, first):
         count = lax.axis_size(axis)
@@ -286,13 +312,14 @@
     z_own, v = pl.pallas_call(
         functools.partial(local, chunks=chunks, unroll=UL),
         out_shape=(pltpu.VMEM((rows, width), F32), pltpu.VMEM((points, rows, LANES), F32)),
-        in_specs=[VMEM] * 2,
+        in_specs=[VMEM] * 4,
         out_specs=(VMEM,) * 2,
+        input_output_aliases={2: 0, 3: 1},
         scratch_shapes=[pltpu.VMEM((UL, 2 * rows, width // chunks), jnp.bfloat16), pltpu.VMEM((rows, LANES), F32)],
         compiler_params=params(8),
         cost_estimate=pl.CostEstimate(flops=8_000_000, bytes_accessed=10_000_000, transcendentals=0),
         name="local",
-    )(here(u_v), jnp.asarray(z_matrix(rows)))
+    )(here(u_v), matrix, here(z_own), here(v))
     return pl.pallas_call(
         functools.partial(finish, chunks=chunks, unroll=UF),
         out_shape=(whole, whole),

time: 22.8 us -> 22.1 us (0.969)
  starting transfers between devices: 9.93 us -> 6.08 us
  waiting for transfers between devices: 0.01 us -> 3.43 us
    ppermute x4, starting transfers between devices: 9.93 us -> 6.08 us  [swap(): return lax.ppermute(x, axis, pairs + [(b, a) for a, b in pairs])]
    ppermute x4, waiting for transfers between devices: 0.01 us -> 3.43 us  [swap(): return lax.ppermute(x, axis, pairs + [(b, a) for a, b in pairs])]
    pallas_call x1, Pallas kernels: 2.76 us -> 0.01 us  [shards(): pl.pallas_call(functools.partial(local, chunks=chunks, unroll=UL), out_sh...]
    pallas_call x1, Pallas kernels: 3.71 us -> 6.21 us  [shards(): pl.pallas_call(functools.partial(summarize, chunks=chunks, unroll=UL), ou...]
  transfers between devices with their start and end apart: 4 -> 4, of which waited for: 0 -> 2; matrix products, arithmetic and copies ran while one was open for 0% -> 0% of each run, Pallas kernels for 12% -> 0%
where the time goes in v3:
time: 22.1 us; the launch traced here: 22 us
  Pallas kernels  11.8 us (53%)
  starting transfers between devices  6.08 us (28%)
  waiting for transfers between devices  3.43 us (16%)
  between operations  0.67 us (3%)
    pallas_call x1, Pallas kernels, shards(): pl.pallas_call(functools.partial(summarize, chunks=chunks, unroll=UL), ou...  6.21 us
    ppermute x4, starting transfers between devices, swap(): return lax.ppermute(x, axis, pairs + [(b, a) for a, b in pairs])  6.08 us
    pallas_call x1, Pallas kernels, shards(): pl.pallas_call(functools.partial(finish, chunks=chunks, unroll=UF), out_s...  5.54 us
    ppermute x4, waiting for transfers between devices, swap(): return lax.ppermute(x, axis, pairs + [(b, a) for a, b in pairs])  3.43 us
  transfers between devices with their start and end apart: 4, of which 2 were waited for; matrix products, arithmetic and copies ran while one was open for 0% of the time, Pallas kernels for 0%

profile of v3, /device:TPU:0, one launch (start us, length us, event | category | flops | bytes accessed | tf_op | source)
XLA Modules:
  0.0 22.0 jit_solution(5048272804123334536)
XLA Ops:
  0.6 0.0 copy-start
  0.6 6.2 %summarize.1 = (f32[96,18432]{1,0:T(8,128)S(1)}, f32[2,18432]{1,0:T(2,128)S(1)}, f32[2,18432]{1,0:T(2,128)S(1)}, f32[96,256]{1,0:T(8,128)S(1)}, f32[104,256]{1,0...) custom-call(f32[96,18432]{1,0:T(8,128)} %u_hbm.1, bf16[192,192]{1,0:T(8,128)(2,1)} %constant.4.clone.m_hbm.matrix), custom_call_target="tpu_custom_call" | custom-call | tf_op jit(solution)/shard_map/summarize/pallas_call | solution.py:279
  6.9 0.1 collective-permute-start
  7.0 4.1 %collective-permute-start.1 = (f32[2,18432]{1,0:T(2,128)S(1)}, f32[2,18432]{1,0:T(2,128)S(1)}, u32[]{:S(2)}, u32[]{:S(2)}) collective-permute-start(f32[2,18432]{1,0:T(2,128)S(1)} %get-tuple-element.17), channel_id=1, source_target_pairs={{1,2},{3,4},{5,6},{7,8},{9,10},{11,12},{13,14},{15,0},{2,1},{4,3},... | collective-permute-start | bytes 442376 | tf_op jit(solution)/shard_map/ppermute | solution.py:307
  11.1 1.9 %collective-permute-start.3 = (f32[104,256]{1,0:T(8,128)S(1)}, f32[104,256]{1,0:T(8,128)S(1)}, u32[]{:S(2)}, u32[]{:S(2)}) collective-permute-start(f32[104,256]{1,0:T(8,128)S(1)} %get-tuple-element.19), channel_id=1, source_target_pairs={{16,32},{48,64},{80,96},{112,0},{32,16},{64,48},{96,80},{0,112},{1... | collective-permute-start | bytes 319496 | tf_op jit(solution)/shard_map/ppermute | solution.py:307
  13.0 0.0 collective-permute-start.2
  13.0 0.0 copy-done
  13.0 0.0 copy-start.1
  13.0 1.3 %collective-permute-done.2.y0 = f32[96,256]{1,0:T(8,128)S(1)} collective-permute-done((f32[96,256]{1,0:T(8,128)S(1)}, f32[96,256]{1,0:T(8,128)S(1)}, u32[]{:S(2)}, u32[]{:S(2)}) %collective-permute-start.2) | collective-permute-done | bytes 98336 | tf_op jit(solution)/shard_map/ppermute | solution.py:307
  14.3 2.1 %collective-permute-done.3.y1 = f32[104,256]{1,0:T(8,128)S(1)} collective-permute-done((f32[104,256]{1,0:T(8,128)S(1)}, f32[104,256]{1,0:T(8,128)S(1)}, u32[]{:S(2)}, u32[]{:S(2)}) %collective-permute-start.3) | collective-permute-done | bytes 106528 | tf_op jit(solution)/shard_map/ppermute | solution.py:307
  16.4 0.0 collective-permute-done.z0
  16.4 0.0 collective-permute-done.1.z1
  16.4 0.0 copy-done.1
  16.4 5.5 %finish.1 = (f32[96,18432]{1,0:T(8,128)}, f32[96,18432]{1,0:T(8,128)}) custom-call(f32[96,18432]{1,0:T(8,128)S(1)} %get-tuple-element.11.u_v, f32[96,18432]{1,0:T(8,128)S(1)} %get-tuple-element.14.z_own, f32[192,96,128]{2,1,0:T(8,128)S(1)} %get-tuple-element.15.v, bf16[96,32]{1,0:T(8,128)(2,1)S(1)} %copy-done.1, f32[2,18432]{1,0:T(2,128)S(1)} %collective-permute-done.z0, ...), custom_call_target="tpu_custom_call" | custom-call | flops 8000000 | bytes 14000000 | tf_op jit(solution)/shard_map/finish/pallas_call | solution.py:323
  (1 shorter events, 0.0 us)
Async XLA Ops:
  0.6 12.3 %copy-start = (bf16[192,192]{1,0:T(8,128)(2,1)S(1)}, bf16[192,192]{1,0:T(8,128)(2,1)}, u32[]{:S(2)}) copy-start(bf16[192,192]{1,0:T(8,128)(2,1)} %constant.4.clone.m_hbm.matrix) | copy-start | bytes 221188
  6.9 9.5 %collective-permute-start = (f32[2,18432]{1,0:T(2,128)S(1)}, f32[2,18432]{1,0:T(2,128)S(1)}, u32[]{:S(2)}, u32[]{:S(2)}) collective-permute-start(f32[2,18432]{1,0:T(2,128)S(1)} %get-tuple-element.16), channel_id=1, source_target_pairs={{0,1},{2,3},{4,5},{6,7},{8,9},{10,11},{12,13},{14,15},{1,0},{3,2},... | collective-permute-start | bytes 442376 | tf_op jit(solution)/shard_map/ppermute | solution.py:307
  7.0 9.4 %collective-permute-start.1 = (f32[2,18432]{1,0:T(2,128)S(1)}, f32[2,18432]{1,0:T(2,128)S(1)}, u32[]{:S(2)}, u32[]{:S(2)}) collective-permute-start(f32[2,18432]{1,0:T(2,128)S(1)} %get-tuple-element.17), channel_id=1, source_target_pairs={{1,2},{3,4},{5,6},{7,8},{9,10},{11,12},{13,14},{15,0},{2,1},{4,3},... | collective-permute-start | bytes 442376 | tf_op jit(solution)/shard_map/ppermute | solution.py:307
  11.1 5.3 %collective-permute-start.3 = (f32[104,256]{1,0:T(8,128)S(1)}, f32[104,256]{1,0:T(8,128)S(1)}, u32[]{:S(2)}, u32[]{:S(2)}) collective-permute-start(f32[104,256]{1,0:T(8,128)S(1)} %get-tuple-element.19), channel_id=1, source_target_pairs={{16,32},{48,64},{80,96},{112,0},{32,16},{64,48},{96,80},{0,112},{1... | collective-permute-start | bytes 319496 | tf_op jit(solution)/shard_map/ppermute | solution.py:307
  13.0 1.3 %collective-permute-start.2 = (f32[96,256]{1,0:T(8,128)S(1)}, f32[96,256]{1,0:T(8,128)S(1)}, u32[]{:S(2)}, u32[]{:S(2)}) collective-permute-start(f32[96,256]{1,0:T(8,128)S(1)} %get-tuple-element.18), channel_id=1, source_target_pairs={{0,16},{32,48},{64,80},{96,112},{16,0},{48,32},{80,64},{112,96},{1... | collective-permute-start | bytes 294920 | tf_op jit(solution)/shard_map/ppermute | solution.py:307
  13.0 3.4 %copy-start.1 = (bf16[96,32]{1,0:T(8,128)(2,1)S(1)}, bf16[96,32]{1,0:T(8,128)(2,1)}, u32[]{:S(2)}) copy-start(bf16[96,32]{1,0:T(8,128)(2,1)} %constant.5.clone.matrix) | copy-start | bytes 18436

commit v4 on v3

--- a/solution.py
+++ b/solution.py
@@ -30,11 +30,25 @@
     return pltpu.roll(x, by, 1)
 
 
+def spread(d, lane):
+    d1, d2, d3 = rolled(d[1], 96), rolled(d[2], 64), rolled(d[3], 32)
+    return jnp.where(lane < 96, d[0], d1), jnp.where(lane < 64, d1, d2), jnp.where(lane < 32, d2, d3)
+
+
+def apart(v0, v1, v2, lane):
+    return [
+        v0,
+        rolled(jnp.where(lane < 96, v1, v0), 32),
+        rolled(jnp.where(lane < 64, v2, v1), 64),
+        rolled(v2, 96),
+    ]
+
+
 def is_even(axis):
     return lax.rem(lax.axis_index(axis), 2) == 0
 
 
-def summarize(u_hbm, m_hbm, u_v, z0, z1, y0, y1, z_own, v, acc_f, acc_b, matrix, rhs, last, sems, *, chunks, unroll):
+def summarize(u_hbm, m_hbm, u_v, z0, z1, y1, y0, z_own, v, acc_f, acc_b, matrix, rhs, last, sems, *, chunks, unroll):
     rows, width = u_v.shape
     wide = width // chunks
     per = wide // BLOCK
@@ -83,9 +97,9 @@
         z0[1:2, lanes] = jnp.where(even_z, e_f, e_b)
         z1[1:2, lanes] = jnp.where(even_z, e_b, e_f)
     lane = lane_index(8)
-    y1[rows:, :] = jnp.zeros((8, 2 * LANES), F32)
-    for g in range(rows // 8):
-        rs = slice(8 * g, 8 * g + 8)
+    half = rows // 2
+
+    def y_ends(rs):
         v0, v1, v2 = (acc_f[rs, k * LANES : (k + 1) * LANES] for k in range(3))
         s = v2 + np.float32(ROOT) * jnp.where(lane < 96, rolled(v1, 96), rolled(v2, 96))
         s = s + np.float32(ROOT**2) * jnp.where(lane < 64, rolled(v0, 64), rolled(v1, 64))
@@ -95,10 +109,15 @@
         s = v0 + np.float32(ROOT) * jnp.where(lane < 32, rolled(v0, 32), rolled(v1, 32))
         s = s + np.float32(ROOT**2) * jnp.where(lane < 64, rolled(v1, 64), rolled(v2, 64))
         s_b, e_b = s + np.float32(ROOT**3) * rolled(v2, 96), u_v[rs, 0:LANES]
-        y0[rs, 0:LANES] = jnp.where(even_y, s_f, s_b)
-        y1[rs, 0:LANES] = jnp.where(even_y, s_b, s_f)
-        y0[rs, LANES:] = jnp.where(even_y, e_f, e_b)
-        y1[rs, LANES:] = jnp.where(even_y, e_b, e_f)
+        return (s_f, e_f), (s_b, e_b)
+
+    for g in range(half // 8):
+        f_0, b_0 = y_ends(slice(8 * g, 8 * g + 8))
+        f_1, b_1 = y_ends(slice(half + 8 * g, half + 8 * g + 8))
+        rs = slice(8 * g, 8 * g + 8)
+        for k, (f, b) in enumerate(zip(spread(f_0 + f_1, lane), spread(b_0 + b_1, lane))):
+            y0[rs, k * LANES : (k + 1) * LANES] = jnp.where(even_y, f, b)
+            y1[rs, k * LANES : (k + 1) * LANES] = jnp.where(even_y, b, f)
     fetch.wait()
 
     @pl.when(at_wrap())
@@ -141,12 +160,7 @@
             for b in range(per):
                 at = c * wide + b * BLOCK
                 v0, v1, v2 = (u_v[rs, at + k * LANES : at + (k + 1) * LANES] * np.float32(EDGE) for k in range(3))
-                points += [
-                    v0,
-                    rolled(jnp.where(lane < 96, v1, v0), 32),
-                    rolled(jnp.where(lane < 64, v2, v1), 64),
-                    rolled(v2, 96),
-                ]
+                points += apart(v0, v1, v2, lane)
             last[rs, :] = points[-1]
             if c < chunks - 1:
                 points.append(u_v[rs, (c + 1) * wide : (c + 1) * wide + LANES] * np.float32(EDGE))
@@ -181,7 +195,7 @@
     return np.concatenate([high, high, low, low], axis=1)
 
 
-def finish(u_v, z_own, v, matrix, z0, z1, y0, y1, dy, dz, y, dy_v, dz_v, halo, rhs, sem_y, sem_z, *, chunks, unroll):
+def finish(u_v, z_own, v, matrix, z0, z1, y1, y0, dy, dz, y, dy_v, dz_v, halo, rhs, sem_y, sem_z, *, chunks, unroll):
     rows, width = u_v.shape
     points = v.shape[0]
     wide = width // chunks
@@ -213,9 +227,15 @@
 
     lax.fori_loop(0, chunks // unroll, z_step, 0)
 
-    y_low = jnp.where(even_y, y1[0:rows, :], y0[...]) * np.float32(EDGE)
-    y_high = jnp.where(even_y, y0[...], y1[0:rows, :]) * np.float32(EDGE)
-    s_low, s_high = y_low[:, :LANES], y_high[:, :LANES]
+    part = rows // 2
+    lane = lane_index(part)
+
+    def y_halo(block):
+        s_0, e_0, s_1, e_1 = apart(*(block[:, k * LANES : (k + 1) * LANES] * np.float32(EDGE) for k in range(3)), lane)
+        return jnp.concatenate([s_0, s_1], axis=0), (e_0, e_1)
+
+    s_low, e_low = y_halo(jnp.where(even_y, y1[...], y0[...]))
+    s_high, e_high = y_halo(jnp.where(even_y, y0[...], y1[...]))
     state = u_v[:, 0:LANES] * np.float32(EDGE) + s_low * np.float32(ROOT - 1 / ROOT)
 
     def forward(i, state):
@@ -231,8 +251,6 @@
     after = state * np.float32(ROOT) - u_last
     far = after * np.float32(ROOT) - s_high
     state = after + far * np.float32(ROOT / (1 - ROOT * ROOT))
-    part = rows // 2
-    lane = lane_index(part)
     state = [state[:part], state[part:]]
     for c in reversed(range(chunks)):
         for b in reversed(range(per)):
@@ -244,12 +262,11 @@
                     state[h] = y[j, rs, :] + state[h] * np.float32(ROOT)
                     d[k] = v[j, rs, :] + state[h] * np.float32(-25 * ROOT)
                     if j == points - 1:
-                        d[k] = d[k] + y_high[rs, LANES:]
+                        d[k] = d[k] + e_high[h]
                     if j == 0:
-                        d[k] = d[k] - y_low[rs, LANES:]
-                d1, d2, d3 = rolled(d[1], 96), rolled(d[2], 64), rolled(d[3], 32)
+                        d[k] = d[k] - e_low[h]
                 at = c * wide + b * BLOCK
-                for k, o in enumerate((jnp.where(lane < 96, d[0], d1), jnp.where(lane < 64, d1, d2), jnp.where(lane < 32, d2, d3))):
+                for k, o in enumerate(spread(d, lane)):
                     dy_v[rs, at + k * LANES : at + (k + 1) * LANES] = o
         copy(dy_v, dy, sem_y, c).start()
 
@@ -276,14 +293,14 @@
     chunks = 12
     whole = jax.ShapeDtypeStruct((rows, width), F32)
     matrix = jnp.asarray(z_matrix(rows))
-    u_v, z0, z1, y0, y1, z_own, v = pl.pallas_call(
+    u_v, z0, z1, y1, y0, z_own, v = pl.pallas_call(
         functools.partial(summarize, chunks=chunks, unroll=UL),
         out_shape=(
             pltpu.VMEM((rows, width), F32),
             jax.ShapeDtypeStruct((2, width), F32),
             jax.ShapeDtypeStruct((2, width), F32),
-            jax.ShapeDtypeStruct((rows, 2 * LANES), F32),
-            jax.ShapeDtypeStruct((rows + 8, 2 * LANES), F32),
+            jax.ShapeDtypeStruct((rows // 2, BLOCK), F32),
+            jax.ShapeDtypeStruct((rows // 2, BLOCK), F32),
             pltpu.VMEM((rows, width), F32),
             pltpu.VMEM((points, rows, LANES), F32),
         ),
@@ -337,7 +354,7 @@
         compiler_params=params(26),
         cost_estimate=pl.CostEstimate(flops=8_000_000, bytes_accessed=14_000_000, transcendentals=0),
         name="finish",
-    )(here(u_v), here(z_own), here(v), jnp.asarray(halo_matrix(rows)), z0, z1, y0, y1)
+    )(here(u_v), here(z_own), here(v), jnp.asarray(halo_matrix(rows)), z0, z1, y1, y0)
 
 
 def solution(mesh):

time: 22.1 us -> 22 us (level)
  waiting for transfers between devices: 3.43 us -> 3.08 us
    ppermute x4, waiting for transfers between devices: 3.43 us -> 3.08 us  [swap(): return lax.ppermute(x, axis, pairs + [(b, a) for a, b in pairs])]
  transfers between devices with their start and end apart: 4 -> 4, of which waited for: 2 -> 1; matrix products, arithmetic and copies ran while one was open for 0% -> 0% of each run, Pallas kernels for 0% -> 0%
where the time goes in v4:
time: 22 us; the launch traced here: 21.8 us
  Pallas kernels  12 us (55%)
  starting transfers between devices  6.06 us (28%)
  waiting for transfers between devices  3.08 us (14%)
  between operations  0.68 us (3%)
    pallas_call x1, Pallas kernels, shards(): pl.pallas_call(functools.partial(summarize, chunks=chunks, unroll=UL), ou...  6.34 us
    ppermute x4, starting transfers between devices, swap(): return lax.ppermute(x, axis, pairs + [(b, a) for a, b in pairs])  6.06 us
    pallas_call x1, Pallas kernels, shards(): pl.pallas_call(functools.partial(finish, chunks=chunks, unroll=UF), out_s...  5.67 us
    ppermute x4, waiting for transfers between devices, swap(): return lax.ppermute(x, axis, pairs + [(b, a) for a, b in pairs])  3.08 us
  transfers between devices with their start and end apart: 4, of which 1 were waited for; matrix products, arithmetic and copies ran while one was open for 0% of the time, Pallas kernels for 0%

profile of v4, /device:TPU:0, one launch (start us, length us, event | category | flops | bytes accessed | tf_op | source)
XLA Modules:
  0.0 21.8 jit_solution(6649529832291436563)
XLA Ops:
  0.6 0.0 copy-start
  0.6 6.3 %summarize.1 = (f32[96,18432]{1,0:T(8,128)S(1)}, f32[2,18432]{1,0:T(2,128)S(1)}, f32[2,18432]{1,0:T(2,128)S(1)}, f32[48,384]{1,0:T(8,128)S(1)}, f32[48,384]{1,0:...) custom-call(f32[96,18432]{1,0:T(8,128)} %u_hbm.1, bf16[192,192]{1,0:T(8,128)(2,1)} %constant.4.clone.m_hbm.matrix), custom_call_target="tpu_custom_call" | custom-call | tf_op jit(solution)/shard_map/summarize/pallas_call | solution.py:296
  7.0 0.1 collective-permute-start
  7.1 4.1 %collective-permute-start.1 = (f32[2,18432]{1,0:T(2,128)S(1)}, f32[2,18432]{1,0:T(2,128)S(1)}, u32[]{:S(2)}, u32[]{:S(2)}) collective-permute-start(f32[2,18432]{1,0:T(2,128)S(1)} %get-tuple-element.17), channel_id=1, source_target_pairs={{1,2},{3,4},{5,6},{7,8},{9,10},{11,12},{13,14},{15,0},{2,1},{4,3},... | collective-permute-start | bytes 442376 | tf_op jit(solution)/shard_map/ppermute | solution.py:324
  11.2 1.9 %collective-permute-start.2 = (f32[48,384]{1,0:T(8,128)S(1)}, f32[48,384]{1,0:T(8,128)S(1)}, u32[]{:S(2)}, u32[]{:S(2)}) collective-permute-start(f32[48,384]{1,0:T(8,128)S(1)} %get-tuple-element.18), channel_id=1, source_target_pairs={{16,32},{48,64},{80,96},{112,0},{32,16},{64,48},{96,80},{0,112},{1... | collective-permute-start | bytes 221192 | tf_op jit(solution)/shard_map/ppermute | solution.py:324
  13.1 0.0 collective-permute-start.3
  13.1 0.0 copy-done
  13.1 0.0 copy-start.1
  13.1 3.1 %collective-permute-done.2.y1 = f32[48,384]{1,0:T(8,128)S(1)} collective-permute-done((f32[48,384]{1,0:T(8,128)S(1)}, f32[48,384]{1,0:T(8,128)S(1)}, u32[]{:S(2)}, u32[]{:S(2)}) %collective-permute-start.2) | collective-permute-done | bytes 73760 | tf_op jit(solution)/shard_map/ppermute | solution.py:324
  16.2 0.0 collective-permute-done.3.y0
  16.2 0.0 collective-permute-done.z0
  16.2 0.0 collective-permute-done.1.z1
  16.2 0.0 copy-done.1
  16.2 5.7 %finish.1 = (f32[96,18432]{1,0:T(8,128)}, f32[96,18432]{1,0:T(8,128)}) custom-call(f32[96,18432]{1,0:T(8,128)S(1)} %get-tuple-element.11.u_v, f32[96,18432]{1,0:T(8,128)S(1)} %get-tuple-element.14.z_own, f32[192,96,128]{2,1,0:T(8,128)S(1)} %get-tuple-element.15.v, bf16[96,32]{1,0:T(8,128)(2,1)S(1)} %copy-done.1, f32[2,18432]{1,0:T(2,128)S(1)} %collective-permute-done.z0, ...), custom_call_target="tpu_custom_call" | custom-call | flops 8000000 | bytes 14000000 | tf_op jit(solution)/shard_map/finish/pallas_call | solution.py:340
  (1 shorter events, 0.0 us)
Async XLA Ops:
  0.6 12.4 %copy-start = (bf16[192,192]{1,0:T(8,128)(2,1)S(1)}, bf16[192,192]{1,0:T(8,128)(2,1)}, u32[]{:S(2)}) copy-start(bf16[192,192]{1,0:T(8,128)(2,1)} %constant.4.clone.m_hbm.matrix) | copy-start | bytes 221188
  7.0 9.2 %collective-permute-start = (f32[2,18432]{1,0:T(2,128)S(1)}, f32[2,18432]{1,0:T(2,128)S(1)}, u32[]{:S(2)}, u32[]{:S(2)}) collective-permute-start(f32[2,18432]{1,0:T(2,128)S(1)} %get-tuple-element.16), channel_id=1, source_target_pairs={{0,1},{2,3},{4,5},{6,7},{8,9},{10,11},{12,13},{14,15},{1,0},{3,2},... | collective-permute-start | bytes 442376 | tf_op jit(solution)/shard_map/ppermute | solution.py:324
  7.1 9.1 %collective-permute-start.1 = (f32[2,18432]{1,0:T(2,128)S(1)}, f32[2,18432]{1,0:T(2,128)S(1)}, u32[]{:S(2)}, u32[]{:S(2)}) collective-permute-start(f32[2,18432]{1,0:T(2,128)S(1)} %get-tuple-element.17), channel_id=1, source_target_pairs={{1,2},{3,4},{5,6},{7,8},{9,10},{11,12},{13,14},{15,0},{2,1},{4,3},... | collective-permute-start | bytes 442376 | tf_op jit(solution)/shard_map/ppermute | solution.py:324
  11.2 5.0 %collective-permute-start.2 = (f32[48,384]{1,0:T(8,128)S(1)}, f32[48,384]{1,0:T(8,128)S(1)}, u32[]{:S(2)}, u32[]{:S(2)}) collective-permute-start(f32[48,384]{1,0:T(8,128)S(1)} %get-tuple-element.18), channel_id=1, source_target_pairs={{16,32},{48,64},{80,96},{112,0},{32,16},{64,48},{96,80},{0,112},{1... | collective-permute-start | bytes 221192 | tf_op jit(solution)/shard_map/ppermute | solution.py:324
  13.1 3.1 %collective-permute-start.3 = (f32[48,384]{1,0:T(8,128)S(1)}, f32[48,384]{1,0:T(8,128)S(1)}, u32[]{:S(2)}, u32[]{:S(2)}) collective-permute-start(f32[48,384]{1,0:T(8,128)S(1)} %get-tuple-element.19), channel_id=1, source_target_pairs={{0,16},{32,48},{64,80},{96,112},{16,0},{48,32},{80,64},{112,96},{1... | collective-permute-start | bytes 221192 | tf_op jit(solution)/shard_map/ppermute | solution.py:324
  13.1 3.1 %copy-start.1 = (bf16[96,32]{1,0:T(8,128)(2,1)S(1)}, bf16[96,32]{1,0:T(8,128)(2,1)}, u32[]{:S(2)}) copy-start(bf16[96,32]{1,0:T(8,128)(2,1)} %constant.5.clone.matrix) | copy-start | bytes 18436

commit v5 on v4

--- a/solution.py
+++ b/solution.py
@@ -17,7 +17,7 @@
 BLOCK = 4 * X
 Q = ROOT**4
 UL = 2
-UF = 4
+UF = 6
 FORWARD = 48
 F32 = jnp.float32
 

time: 22 us -> 21.8 us (level)
  no operation moved by 1% of the time
where the time goes in v5:
time: 21.8 us; the launch traced here: 21.7 us
  Pallas kernels  11.9 us (55%)
  starting transfers between devices  6.06 us (28%)
  waiting for transfers between devices  3.08 us (14%)
  between operations  0.68 us (3%)
    pallas_call x1, Pallas kernels, shards(): pl.pallas_call(functools.partial(summarize, chunks=chunks, unroll=UL), ou...  6.34 us
    ppermute x4, starting transfers between devices, swap(): return lax.ppermute(x, axis, pairs + [(b, a) for a, b in pairs])  6.06 us
    pallas_call x1, Pallas kernels, shards(): pl.pallas_call(functools.partial(finish, chunks=chunks, unroll=UF), out_s...  5.52 us
    ppermute x4, waiting for transfers between devices, swap(): return lax.ppermute(x, axis, pairs + [(b, a) for a, b in pairs])  3.08 us
  transfers between devices with their start and end apart: 4, of which 1 were waited for; matrix products, arithmetic and copies ran while one was open for 0% of the time, Pallas kernels for 0%

profile of v5, /device:TPU:0, one launch (start us, length us, event | category | flops | bytes accessed | tf_op | source)
XLA Modules:
  0.0 21.7 jit_solution(6456501689652684851)
XLA Ops:
  0.6 0.0 copy-start
  0.6 6.3 %summarize.1 = (f32[96,18432]{1,0:T(8,128)S(1)}, f32[2,18432]{1,0:T(2,128)S(1)}, f32[2,18432]{1,0:T(2,128)S(1)}, f32[48,384]{1,0:T(8,128)S(1)}, f32[48,384]{1,0:...) custom-call(f32[96,18432]{1,0:T(8,128)} %u_hbm.1, bf16[192,192]{1,0:T(8,128)(2,1)} %constant.4.clone.m_hbm.matrix), custom_call_target="tpu_custom_call" | custom-call | tf_op jit(solution)/shard_map/summarize/pallas_call | solution.py:296
  7.0 0.1 collective-permute-start
  7.1 4.1 %collective-permute-start.1 = (f32[2,18432]{1,0:T(2,128)S(1)}, f32[2,18432]{1,0:T(2,128)S(1)}, u32[]{:S(2)}, u32[]{:S(2)}) collective-permute-start(f32[2,18432]{1,0:T(2,128)S(1)} %get-tuple-element.17), channel_id=1, source_target_pairs={{1,2},{3,4},{5,6},{7,8},{9,10},{11,12},{13,14},{15,0},{2,1},{4,3},... | collective-permute-start | bytes 442376 | tf_op jit(solution)/shard_map/ppermute | solution.py:324
  11.2 1.9 %collective-permute-start.2 = (f32[48,384]{1,0:T(8,128)S(1)}, f32[48,384]{1,0:T(8,128)S(1)}, u32[]{:S(2)}, u32[]{:S(2)}) collective-permute-start(f32[48,384]{1,0:T(8,128)S(1)} %get-tuple-element.18), channel_id=1, source_target_pairs={{16,32},{48,64},{80,96},{112,0},{32,16},{64,48},{96,80},{0,112},{1... | collective-permute-start | bytes 221192 | tf_op jit(solution)/shard_map/ppermute | solution.py:324
  13.1 0.0 collective-permute-start.3
  13.1 0.0 copy-done
  13.1 0.0 copy-start.1
  13.1 3.1 %collective-permute-done.2.y1 = f32[48,384]{1,0:T(8,128)S(1)} collective-permute-done((f32[48,384]{1,0:T(8,128)S(1)}, f32[48,384]{1,0:T(8,128)S(1)}, u32[]{:S(2)}, u32[]{:S(2)}) %collective-permute-start.2) | collective-permute-done | bytes 73760 | tf_op jit(solution)/shard_map/ppermute | solution.py:324
  16.2 0.0 collective-permute-done.3.y0
  16.2 0.0 collective-permute-done.z0
  16.2 0.0 collective-permute-done.1.z1
  16.2 0.0 copy-done.1
  16.2 5.5 %finish.1 = (f32[96,18432]{1,0:T(8,128)}, f32[96,18432]{1,0:T(8,128)}) custom-call(f32[96,18432]{1,0:T(8,128)S(1)} %get-tuple-element.11.u_v, f32[96,18432]{1,0:T(8,128)S(1)} %get-tuple-element.14.z_own, f32[192,96,128]{2,1,0:T(8,128)S(1)} %get-tuple-element.15.v, bf16[96,32]{1,0:T(8,128)(2,1)S(1)} %copy-done.1, f32[2,18432]{1,0:T(2,128)S(1)} %collective-permute-done.z0, ...), custom_call_target="tpu_custom_call" | custom-call | flops 8000000 | bytes 14000000 | tf_op jit(solution)/shard_map/finish/pallas_call | solution.py:340
  (1 shorter events, 0.0 us)
Async XLA Ops:
  0.6 12.4 %copy-start = (bf16[192,192]{1,0:T(8,128)(2,1)S(1)}, bf16[192,192]{1,0:T(8,128)(2,1)}, u32[]{:S(2)}) copy-start(bf16[192,192]{1,0:T(8,128)(2,1)} %constant.4.clone.m_hbm.matrix) | copy-start | bytes 221188
  7.0 9.2 %collective-permute-start = (f32[2,18432]{1,0:T(2,128)S(1)}, f32[2,18432]{1,0:T(2,128)S(1)}, u32[]{:S(2)}, u32[]{:S(2)}) collective-permute-start(f32[2,18432]{1,0:T(2,128)S(1)} %get-tuple-element.16), channel_id=1, source_target_pairs={{0,1},{2,3},{4,5},{6,7},{8,9},{10,11},{12,13},{14,15},{1,0},{3,2},... | collective-permute-start | bytes 442376 | tf_op jit(solution)/shard_map/ppermute | solution.py:324
  7.1 9.1 %collective-permute-start.1 = (f32[2,18432]{1,0:T(2,128)S(1)}, f32[2,18432]{1,0:T(2,128)S(1)}, u32[]{:S(2)}, u32[]{:S(2)}) collective-permute-start(f32[2,18432]{1,0:T(2,128)S(1)} %get-tuple-element.17), channel_id=1, source_target_pairs={{1,2},{3,4},{5,6},{7,8},{9,10},{11,12},{13,14},{15,0},{2,1},{4,3},... | collective-permute-start | bytes 442376 | tf_op jit(solution)/shard_map/ppermute | solution.py:324
  11.2 5.0 %collective-permute-start.2 = (f32[48,384]{1,0:T(8,128)S(1)}, f32[48,384]{1,0:T(8,128)S(1)}, u32[]{:S(2)}, u32[]{:S(2)}) collective-permute-start(f32[48,384]{1,0:T(8,128)S(1)} %get-tuple-element.18), channel_id=1, source_target_pairs={{16,32},{48,64},{80,96},{112,0},{32,16},{64,48},{96,80},{0,112},{1... | collective-permute-start | bytes 221192 | tf_op jit(solution)/shard_map/ppermute | solution.py:324
  13.1 3.1 %collective-permute-start.3 = (f32[48,384]{1,0:T(8,128)S(1)}, f32[48,384]{1,0:T(8,128)S(1)}, u32[]{:S(2)}, u32[]{:S(2)}) collective-permute-start(f32[48,384]{1,0:T(8,128)S(1)} %get-tuple-element.19), channel_id=1, source_target_pairs={{0,16},{32,48},{64,80},{96,112},{16,0},{48,32},{80,64},{112,96},{1... | collective-permute-start | bytes 221192 | tf_op jit(solution)/shard_map/ppermute | solution.py:324
  13.1 3.1 %copy-start.1 = (bf16[96,32]{1,0:T(8,128)(2,1)S(1)}, bf16[96,32]{1,0:T(8,128)(2,1)}, u32[]{:S(2)}) copy-start(bf16[96,32]{1,0:T(8,128)(2,1)} %constant.5.clone.matrix) | copy-start | bytes 18436
